TPU v7x, 256 devices: a whole 4x4x8 slice. The times are simulated.
256 devices in a mesh: row: 32 (over y, x, core), col: 8 (over z).
Axes of the slice: x: 4, y: 4, z: 8, core: 2. Of those that a mesh axis runs over, the one named last changes fastest.
Arguments:
- root_inv: float32 [4096, 4096], P('row', 'col'), as said below
- level1_inv: float32 [1024, 2, 1024], P('row', None, 'col'), as said below
- level1_panel: float32 [4096, 2, 1024], P('row', None, 'col'), may hold values from -0.0625 to 0.0625
- child_inv: float32 [4, 1024, 1024], P(None, 'row', 'col'), as said below
- child_panel: float32 [4, 2048, 1024], P(None, 'row', 'col'), may hold values from -0.09375 to 0.09375
- child_width: int32 [4], replicated, may hold values from 1 to 1024, 2560 in all
- child_parent: int32 [4], replicated, may hold values from 0 to 1, as said below
- child_blocks: int32 [4, 64], replicated, may hold values from 0 to 159, as said below
Outputs:
- leverage_root: float32 [4096], P('row')
- leverage_parent: float32 [2, 1024], P(None, 'row')
- leverage_child: float32 [4, 1024], P(None, 'col')
Inputs may be any that keep to these rules, and one draw needn't show every extreme that they name: `root_inv`: zero above the diagonal. `level1_inv`: each [:, k, :] is zero above the diagonal. `child_inv`: each [j] is zero above the diagonal. `child_width`: the widths sum to 2560. `child_parent`: each parent has exactly two of the 4 children. `child_blocks`: each row lists 64 distinct numbers in increasing order, 0 and 159 among them; numbers below 128 name blocks of the root, the others blocks of the supernode's parent.
All inputs are finite; a program needn't handle non-finite values.
Results may differ from a plain program's by a relative error of at most 0.0001.
Values sent between devices are 32-bit elements; how exact they have to be, the bound alone decides.
No kernel may reach another device: no remote copies, remote signals or barrier semaphores. Data moves between devices by JAX's collectives and lax.ppermute only.
A program may use at most 128 MiB of HBM per device.

v0:
```python
import jax
import jax.numpy as jnp
from jax import lax
from jax.sharding import PartitionSpec as P

BLOCK_ROWS = 32


highest = lax.Precision.HIGHEST


def product(former, latter):
    return jnp.dot(former, latter, precision=highest, preferred_element_type=jnp.float32)


def inner_rows(former, latter):
    return lax.dot_general(
        former,
        latter,
        (((0,), (0,)), ((), ())),
        precision=highest,
        preferred_element_type=jnp.float32,
    )


def diagonal_part(matrix, offset):
    square = lax.dynamic_slice_in_dim(matrix, offset, matrix.shape[0], 1)
    return jnp.diagonal(square)


def body(
    root_inv,
    level1_inv,
    level1_panel,
    child_inv,
    child_panel,
    child_width,
    child_parent,
    child_blocks,
):
    row_index = lax.axis_index("row")
    col_index = lax.axis_index("col")
    root_local = root_inv.shape[0]
    parent_local = level1_inv.shape[0]
    root_full, inverse_full = (
        lax.all_gather(root_inv, "col", axis=1, tiled=True),
        lax.all_gather(level1_inv, "col", axis=2, tiled=True),
    )
    root_width = root_full.shape[1]
    root_block = lax.psum_scatter(
        inner_rows(root_full, root_inv), "row", scatter_dimension=0, tiled=True
    )
    root_cov = lax.all_gather(root_block, "col", axis=1, tiled=True)
    leverage_root = diagonal_part(root_cov, row_index * root_local)
    panel_flat = level1_panel.reshape(root_local, -1)
    cross_flat = lax.psum_scatter(
        inner_rows(root_cov, panel_flat), "row", scatter_dimension=0, tiled=True
    )
    cross_block = cross_flat.reshape(level1_panel.shape)
    cross_rows = lax.all_gather(cross_block, "col", axis=2, tiled=True)
    cross_cols = lax.all_to_all(cross_rows, "row", split_axis=2, concat_axis=0, tiled=True)
    first = jnp.einsum("ikn,ikm->nkm", cross_rows, level1_panel, precision=highest)
    second = jnp.einsum("akn,akm->nkm", inverse_full, level1_inv, precision=highest)
    parent_block = lax.psum_scatter(first + second, "row", scatter_dimension=0, tiled=True)
    parent_cov = lax.all_gather(parent_block, "col", axis=2, tiled=True)
    leverage_parent = jnp.stack(
        [
            diagonal_part(parent_cov[:, member, :], row_index * parent_local)
            for member in range(parent_cov.shape[1])
        ]
    )
    child_local = child_inv.shape[1]
    child_part = child_inv.shape[2]
    root_blocks = root_local // BLOCK_ROWS
    parent_blocks = parent_local // BLOCK_ROWS
    owned = jnp.concatenate(
        [
            row_index * root_blocks + jnp.arange(root_blocks, dtype=jnp.int32),
            root_width // BLOCK_ROWS
            + row_index * parent_blocks
            + jnp.arange(parent_blocks, dtype=jnp.int32),
        ]
    )
    col_global = col_index * child_part + jnp.arange(child_part, dtype=jnp.int32)
    row_global = row_index * child_local + jnp.arange(child_local, dtype=jnp.int32)
    offsets = jnp.arange(BLOCK_ROWS, dtype=jnp.int32)
    partials = []
    for member in range(child_panel.shape[0]):
        width = child_width[member]
        live_cols = (col_global < width).astype(jnp.float32)
        live_rows = (row_global < width).astype(jnp.float32)
        normal = child_panel[member] * live_cols[None, :]
        factor = child_inv[member] * live_rows[:, None] * live_cols[None, :]
        parent = child_parent[member]
        cross_mine = lax.dynamic_index_in_dim(cross_rows, parent, 1, keepdims=False)
        cross_theirs = lax.dynamic_index_in_dim(cross_cols, parent, 1, keepdims=False)
        diagonal_mine = lax.dynamic_index_in_dim(parent_cov, parent, 1, keepdims=False)
        ancestor = jnp.concatenate(
            [
                jnp.concatenate([root_cov, -cross_mine], axis=1),
                jnp.concatenate([-cross_theirs.T, diagonal_mine], axis=1),
            ],
            axis=0,
        )
        blocks = child_blocks[member]
        slots = (blocks[:, None] * BLOCK_ROWS + offsets[None, :]).reshape(-1)
        picked = jnp.take(ancestor, slots, axis=1)
        selector = (owned[:, None] == blocks[None, :]).astype(jnp.float32)
        normal_full = lax.all_gather(normal, "row", axis=0, tiled=True)
        owned_rows = product(selector, normal_full.reshape(blocks.shape[0], -1)).reshape(
            -1, child_part
        )
        image = lax.psum_scatter(
            inner_rows(picked, owned_rows), "row", scatter_dimension=0, tiled=True
        )
        contribution = jnp.sum(normal * image, axis=0)
        partials.append(contribution + jnp.sum(factor * factor, axis=0))
    leverage_child = lax.psum(jnp.stack(partials), "row")
    return (leverage_root, leverage_parent, leverage_child)


def solution(mesh):
    placed = (
        P("row", "col"),
        P("row", None, "col"),
        P("row", None, "col"),
        P(None, "row", "col"),
        P(None, "row", "col"),
        P(),
        P(),
        P(),
    )
    return jax.shard_map(
        body,
        mesh=mesh,
        in_specs=placed,
        out_specs=(P("row"), P(None, "row"), P(None, "col")),
        check_vma=False,
    )
```

profile of v0, /device:TPU:1, one launch (start us, length us, event | category | flops | bytes accessed | tf_op | source)
XLA Modules:
  0.0 1061.2 jit_solution(14907236986459807811)
XLA Ops:
  7.9 43.1 %all-gather.8.cloned.1.call-done = f32[128,4096]{1,0:T(8,128)} async-done(((f32[128,512]{1,0:T(8,128)}), f32[128,4096]{1,0:T(8,128)}) %all-gather.8.cloned.1.call-update) | async-done | bytes 2097168 | tf_op jit(solution)/shard_map/all_gather | solution.py:46
  51.0 10.2 fusion.68
  61.4 101.0 %reduce-scatter.8.cloned.1.call-done = f32[128,512]{1,0:T(8,128)} async-done(((f32[4096,512]{1,0:T(8,128)}), f32[128,512]{1,0:T(8,128)}) %reduce-scatter.8.cloned.1.call-update) | async-done | bytes 262160 | tf_op jit(solution)/shard_map/reduce_scatter | solution.py:50
  162.4 40.4 %all-gather.10.cloned.1.call-done = f32[128,4096]{1,0:T(8,128)} async-done(((f32[128,512]{1,0:T(8,128)}), f32[128,4096]{1,0:T(8,128)}) %all-gather.10.cloned.1.call-update) | async-done | bytes 2097168 | tf_op jit(solution)/shard_map/all_gather | solution.py:53
  202.9 7.0 fusion.25
  210.0 90.3 %reduce-scatter.10.cloned.1.call-done = f32[128,256]{1,0:T(8,128)} async-done(((f32[4096,256]{1,0:T(8,128)}), f32[128,256]{1,0:T(8,128)}) %reduce-scatter.10.cloned.1.call-update) | async-done | bytes 131088 | tf_op jit(solution)/shard_map/reduce_scatter | solution.py:56
  306.1 21.0 %all_gather.30 = f32[32,2,1024]{2,0,1:T(8,128)S(1)} all-gather(f32[32,2,128]{2,0,1:T(8,128)S(1)} %copy.39), channel_id=1, replica_groups=mesh['row'=32,'col'=8] {'col'}, dimensions={2}, use_global_device_ids=true | all-gather | bytes 294912 | tf_op jit(solution)/shard_map/all_gather | solution.py:47
  328.9 10.7 %all-gather.12.cloned.1.call-done = f32[128,2,1024]{2,0,1:T(8,128)} async-done(((f32[128,2,128]{2,0,1:T(8,128)}), f32[128,2,1024]{2,0,1:T(8,128)}) %all-gather.12.cloned.1.call-update) | async-done | bytes 1048592 | tf_op jit(solution)/shard_map/all_gather | solution.py:60
  349.7 11.2 %all-to-all-start = ((f32[128,2,1024]{0,1,2:T(2,128)}), f32[128,2,1024]{0,1,2:T(2,128)S(1)}, u32[]{:S(2)}, u32[]{:S(2)}) async-start(f32[128,2,1024]{0,1,2:T(2,128)} %copy.41), calls=%async_computation.3 | async-start | bytes 2097152 | tf_op jit(solution)/shard_map/all_to_all | solution.py:61
  369.0 29.6 %all-gather.20.cloned.1.call-done = f32[2048,128]{1,0:T(8,128)} async-done(((f32[64,128]{1,0:T(8,128)}), f32[2048,128]{1,0:T(8,128)}) %all-gather.20.cloned.1.call-update) | async-done | bytes 1048592 | tf_op jit(solution)/shard_map/all_gather | solution.py:109
  404.1 80.8 %reduce-scatter.12.cloned.1.call-done = f32[32,2,128]{2,0,1:T(8,128)} async-done(((f32[1024,2,128]{2,0,1:T(8,128)}), f32[32,2,128]{2,0,1:T(8,128)}) %reduce-scatter.12.cloned.1.call-update) | async-done | bytes 32784 | tf_op jit(solution)/shard_map/reduce_scatter | solution.py:64
  484.8 20.4 %all_gather.31 = f32[32,2,1024]{2,0,1:T(8,128)S(1)} all-gather(f32[32,2,128]{2,0,1:T(8,128)} %reduce-scatter.12.cloned.1.call-done), channel_id=1, replica_groups=mesh['row'=32,'col'=8] {'col'}, dimensions={2}, use_global_device_ids=true | all-gather | bytes 294912 | tf_op jit(solution)/shard_map/all_gather | solution.py:65
  506.1 7.4 fusion
  518.9 11.1 %gather_fusion.6 = f32[2048,160]{1,0:T(8,128)} fusion(f32[160,5120]{0,1:T(8,128)} %copy.47, s32[2048]{0:T(1024)S(1)} %fusion.44), kind=kCustom, calls=%fused_computation.3.clone | custom fusion | bytes 2629632 | tf_op jit(solution)/shard_map/jit(_take)/gather | solution.py:107
  546.6 11.1 %gather_fusion.5 = f32[2048,160]{1,0:T(8,128)} fusion(f32[160,5120]{0,1:T(8,128)} %copy.46, s32[2048]{0:T(1024)S(1)} %fusion.43), kind=kCustom, calls=%fused_computation.2.clone | custom fusion | bytes 2629632 | tf_op jit(solution)/shard_map/jit(_take)/gather | solution.py:107
  562.7 24.4 %all-gather.16.cloned.1.call-done = f32[2048,128]{1,0:T(8,128)} async-done(((f32[64,128]{1,0:T(8,128)}), f32[2048,128]{1,0:T(8,128)}) %all-gather.16.cloned.1.call-update) | async-done | bytes 1048592 | tf_op jit(solution)/shard_map/all_gather | solution.py:109
  596.7 11.1 %gather_fusion.4 = f32[2048,160]{1,0:T(8,128)} fusion(f32[160,5120]{0,1:T(8,128)} %copy.45, s32[2048]{0:T(1024)S(1)} %fusion.42), kind=kCustom, calls=%fused_computation.1.clone | custom fusion | bytes 2629632 | tf_op jit(solution)/shard_map/jit(_take)/gather | solution.py:107
  614.9 22.1 %all-gather.14.cloned.1.call-done = f32[2048,128]{1,0:T(8,128)} async-done(((f32[64,128]{1,0:T(8,128)}), f32[2048,128]{1,0:T(8,128)}) %all-gather.14.cloned.1.call-update) | async-done | bytes 1048592 | tf_op jit(solution)/shard_map/all_gather | solution.py:109
  644.9 9.1 gather_fusion.3
  662.6 61.1 %reduce-scatter.20.cloned.1.call-done = f32[64,128]{1,0:T(8,128)} async-done(((f32[2048,128]{1,0:T(8,128)}), f32[64,128]{1,0:T(8,128)}) %reduce-scatter.20.cloned.1.call-update) | async-done | bytes 32784 | tf_op jit(solution)/shard_map/reduce_scatter | solution.py:113
  724.5 87.4 %reduce-scatter.18.cloned.1.call-done = f32[64,128]{1,0:T(8,128)} async-done(((f32[2048,128]{1,0:T(8,128)}), f32[64,128]{1,0:T(8,128)}) %reduce-scatter.18.cloned.1.call-update) | async-done | bytes 32784 | tf_op jit(solution)/shard_map/reduce_scatter | solution.py:113
  812.7 88.0 %reduce-scatter.16.cloned.1.call-done = f32[64,128]{1,0:T(8,128)} async-done(((f32[2048,128]{1,0:T(8,128)}), f32[64,128]{1,0:T(8,128)}) %reduce-scatter.16.cloned.1.call-update) | async-done | bytes 32784 | tf_op jit(solution)/shard_map/reduce_scatter | solution.py:113
  901.5 87.4 %reduce-scatter.14.cloned.1.call-done = f32[64,128]{1,0:T(8,128)} async-done(((f32[2048,128]{1,0:T(8,128)}), f32[64,128]{1,0:T(8,128)}) %reduce-scatter.14.cloned.1.call-update) | async-done | bytes 32784 | tf_op jit(solution)/shard_map/reduce_scatter | solution.py:113
  989.7 64.9 %psum.7 = f32[4,128]{1,0:T(4,128)} all-reduce(f32[4,128]{1,0:T(4,128)S(1)} %pad_maximum_fusion.4), channel_id=1, replica_groups=mesh['row'=32,'col'=8] {'row'}, use_global_device_ids=true, to_apply=%region_15.17 | all-reduce | flops 512 | bytes 4096 | tf_op jit(solution)/shard_map/psum | solution.py:118
  (158 shorter events, 88.0 us)
Async XLA Ops:
  7.2 43.9 %all-gather.8.cloned.1.call-start = ((), (), s32[]{:S(2)}) async-start(), calls=%async_computation.8 | async-start | bytes 2359296 | tf_op jit(solution)/shard_map/all_gather | solution.py:46
  7.9 154.5 %reduce-scatter.8.cloned.1.call-start = ((), (), s32[]{:S(2)}) async-start(), calls=%async_computation.9 | async-start | bytes 8650752 | tf_op jit(solution)/shard_map/reduce_scatter | solution.py:50
  61.3 141.6 %copy-start.1 = (f32[128,2,128]{2,1,0:T(2,128)S(1)}, f32[128,2,128]{2,1,0:T(2,128)}, u32[]{:S(2)}) copy-start(f32[128,2,128]{2,1,0:T(2,128)} %param.12) | copy-start | bytes 393220
  61.3 141.5 %all-gather.10.cloned.1.call-start = ((), (), s32[]{:S(2)}) async-start(), calls=%async_computation.10 | async-start | bytes 2359296 | tf_op jit(solution)/shard_map/all_gather | solution.py:53
  162.4 137.9 %reduce-scatter.10.cloned.1.call-start = ((), (), s32[]{:S(2)}) async-start(), calls=%async_computation.11 | async-start | bytes 4325376 | tf_op jit(solution)/shard_map/reduce_scatter | solution.py:56
  209.9 92.2 %copy-start.12 = (s32[4]{0:T(128)S(1)}, s32[4]{0:T(128)}, u32[]{:S(2)}) copy-start(s32[4]{0:T(128)} %param.15) | copy-start | bytes 52
  209.9 95.4 %copy-start.8 = (f32[4,64,128]{2,1,0:T(8,128)S(1)}, f32[4,64,128]{2,1,0:T(8,128)}, u32[]{:S(2)}) copy-start(f32[4,64,128]{2,1,0:T(8,128)} %param.14) | copy-start | bytes 393220
  209.9 96.2 %copy-start.9 = (f32[32,2,128]{2,1,0:T(2,128)S(1)}, f32[32,2,128]{2,1,0:T(2,128)}, u32[]{:S(2)}) copy-start(f32[32,2,128]{2,1,0:T(2,128)} %param.11) | copy-start | bytes 98308
  209.9 129.7 %all-gather.12.cloned.1.call-start = ((), (), s32[]{:S(2)}) async-start(), calls=%async_computation.12 | async-start | bytes 1179648 | tf_op jit(solution)/shard_map/all_gather | solution.py:60
  302.0 96.5 %all-gather.20.cloned.1.call-start = ((), (), s32[]{:S(2)}) async-start(), calls=%async_computation.20 | async-start | bytes 1081344 | tf_op jit(solution)/shard_map/all_gather | solution.py:109
  306.0 178.8 %reduce-scatter.12.cloned.1.call-start = ((), (), s32[]{:S(2)}) async-start(), calls=%async_computation.13 | async-start | bytes 1081344 | tf_op jit(solution)/shard_map/reduce_scatter | solution.py:64
  343.8 193.2 %all-gather.18.cloned.1.call-start = ((), (), s32[]{:S(2)}) async-start(), calls=%async_computation.18 | async-start | bytes 1081344 | tf_op jit(solution)/shard_map/all_gather | solution.py:109
  344.5 242.6 %all-gather.16.cloned.1.call-start = ((), (), s32[]{:S(2)}) async-start(), calls=%async_computation.16 | async-start | bytes 1081344 | tf_op jit(solution)/shard_map/all_gather | solution.py:109
  345.2 291.8 %all-gather.14.cloned.1.call-start = ((), (), s32[]{:S(2)}) async-start(), calls=%async_computation.14 | async-start | bytes 1081344 | tf_op jit(solution)/shard_map/all_gather | solution.py:109
  349.7 52.8 %all-to-all-start = ((f32[128,2,1024]{0,1,2:T(2,128)}), f32[128,2,1024]{0,1,2:T(2,128)S(1)}, u32[]{:S(2)}, u32[]{:S(2)}) async-start(f32[128,2,1024]{0,1,2:T(2,128)} %copy.41), calls=%async_computation.3 | async-start | bytes 2097152 | tf_op jit(solution)/shard_map/all_to_all | solution.py:61
  360.9 362.8 %reduce-scatter.20.cloned.1.call-start = ((), (), s32[]{:S(2)}) async-start(), calls=%async_computation.21 | async-start | bytes 1081344 | tf_op jit(solution)/shard_map/reduce_scatter | solution.py:113
  534.5 277.5 %reduce-scatter.18.cloned.1.call-start = ((), (), s32[]{:S(2)}) async-start(), calls=%async_computation.19 | async-start | bytes 1081344 | tf_op jit(solution)/shard_map/reduce_scatter | solution.py:113
  562.2 27.3 %copy-start.23 = (s32[64]{0:T(128)S(1)}, s32[64]{0:T(128)}, u32[]{:S(2)}) copy-start(s32[64]{0:T(128)} %get-tuple-element.35) | copy-start | bytes 772
  562.2 338.5 %reduce-scatter.16.cloned.1.call-start = ((), (), s32[]{:S(2)}) async-start(), calls=%async_computation.17 | async-start | bytes 1081344 | tf_op jit(solution)/shard_map/reduce_scatter | solution.py:113
  612.3 376.7 %reduce-scatter.14.cloned.1.call-start = ((), (), s32[]{:S(2)}) async-start(), calls=%async_computation.15 | async-start | bytes 1081344 | tf_op jit(solution)/shard_map/reduce_scatter | solution.py:113
  657.0 66.8 %copy-start.6 = (f32[64,128]{1,0:T(8,128)S(1)}, f32[64,128]{1,0:T(8,128)}, u32[]{:S(2)}) copy-start(f32[64,128]{1,0:T(8,128)} %get-tuple-element.28) | copy-start | bytes 98308
  657.0 155.0 %copy-start.5 = (f32[64,128]{1,0:T(8,128)S(1)}, f32[64,128]{1,0:T(8,128)}, u32[]{:S(2)}) copy-start(f32[64,128]{1,0:T(8,128)} %get-tuple-element.29) | copy-start | bytes 98308
  657.0 243.7 %copy-start.4 = (f32[64,128]{1,0:T(8,128)S(1)}, f32[64,128]{1,0:T(8,128)}, u32[]{:S(2)}) copy-start(f32[64,128]{1,0:T(8,128)} %get-tuple-element.27) | copy-start | bytes 98308
  657.0 332.0 %copy-start.3 = (f32[64,128]{1,0:T(8,128)S(1)}, f32[64,128]{1,0:T(8,128)}, u32[]{:S(2)}) copy-start(f32[64,128]{1,0:T(8,128)} %get-tuple-element.26) | copy-start | bytes 98308
  (18 other events, 212.9 us)
Sparse Core Ops, SparseCore 0:
  9.8 41.2 all-gather.7
  61.4 100.8 reduce-scatter.7
  164.3 38.5 all-gather.9
  210.0 90.1 reduce-scatter.9
  302.1 37.4 all-gather.11
  342.0 56.4 all-gather.19
  402.4 82.4 reduce-scatter.11
  487.7 49.2 all-gather.17
  539.9 47.1 all-gather.15
  589.8 47.1 all-gather.13
  641.3 82.3 reduce-scatter.19
  727.4 84.5 reduce-scatter.17
  816.2 84.4 reduce-scatter.15
  904.3 84.5 reduce-scatter.13
where the time goes:
time: 1060 us
  waiting for transfers between devices  771 us (73%)
  blocking collectives  106 us (10%)
  local copies, waits for them, and re-layouts  83.2 us (8%)
  matrix products  44.8 us (4%)
  between operations  22.2 us (2%)
  other arithmetic  21.2 us (2%)
  starting transfers between devices  12 us (1%)
    reduce_scatter x4, waiting for transfers between devices, body(): lax.psum_scatter(inner_rows(picked, owned_rows), 'row', scatter_dimension...  324 us
    reduce_scatter x1, waiting for transfers between devices, body(): lax.psum_scatter(inner_rows(root_full, root_inv), 'row', scatter_dimensio...  101 us
    reduce_scatter x1, waiting for transfers between devices, body(): lax.psum_scatter(inner_rows(root_cov, panel_flat), 'row', scatter_dimensi...  90.3 us
    reduce_scatter x1, waiting for transfers between devices, body(): lax.psum_scatter(first + second, 'row', scatter_dimension=0, tiled=True)  80.8 us
    all_gather x4, waiting for transfers between devices, body(): normal_full = lax.all_gather(normal, 'row', axis=0, tiled=True)  78.4 us
    psum x1, blocking collectives, body(): leverage_child = lax.psum(jnp.stack(partials), 'row')  64.9 us
    all_gather x1, waiting for transfers between devices, body(): lax.all_gather(root_inv, 'col', axis=1, tiled=True)  43.1 us
    gather x4, local copies, waits for them, and re-layouts, body(): picked = jnp.take(ancestor, slots, axis=1)  42.4 us
  transfers between devices with their start and end apart: 15, of which 14 were waited for; matrix products, arithmetic and copies ran while one was open for 12% of the time, Pallas kernels for 0%

commit v1 on v0

v1 whole, which is shorter than its diff:
```python
import jax
import jax.numpy as jnp
from jax import lax
from jax.experimental import pallas as pl
from jax.experimental.pallas import tpu as pltpu
from jax.sharding import PartitionSpec as P

BLOCK_ROWS = 32
PAIRS = [(i, i ^ 1) for i in range(32)]
SAME_CORE = [[2 * m + k for m in range(16)] for k in range(2)]
f32 = jnp.float32
bf16 = jnp.bfloat16

VMEM = pl.BlockSpec(memory_space=pltpu.VMEM)
SMEM = pl.BlockSpec(memory_space=pltpu.SMEM)
PARAMS = pltpu.CompilerParams(vmem_limit_bytes=48 * 1024 * 1024)


def call(kernel, outs, specs, flops, nbytes, scratch=()):
    return pl.pallas_call(
        kernel,
        out_shape=[jax.ShapeDtypeStruct(s, d) for s, d in outs],
        in_specs=specs,
        out_specs=[VMEM] * len(outs),
        scratch_shapes=list(scratch),
        compiler_params=PARAMS,
        cost_estimate=pl.CostEstimate(flops=flops, bytes_accessed=nbytes, transcendentals=0),
    )


def split(x):
    high = x.astype(bf16)
    return high, (x - high.astype(f32)).astype(bf16)


def dot(a, b):
    return jnp.dot(a, b, preferred_element_type=f32)


def squares(x):
    return jnp.sum(x * x, axis=0, keepdims=True)


def kids_of(parents, which):
    hit = [parents[j] == which for j in range(4)]
    first = jnp.where(hit[0], 0, jnp.where(hit[1], 1, 2))
    second = jnp.where(hit[3], 3, jnp.where(hit[2], 2, 1))
    return first, second


def pack_kernel(ids, parents, widths, panel, level1, child, keep, give):
    for out, which in ((keep, ids[0]), (give, 1 - ids[0])):
        out[0:128, :] = panel[pl.ds(which, 128, stride=2), :]
        lanes = ids[1] * 128 + lax.broadcasted_iota(jnp.int32, (64, 128), 1)
        for place, kid in enumerate(kids_of(parents, which)):
            live = lanes < widths[kid]
            out[128 + 64 * place : 192 + 64 * place, :] = jnp.where(live, child[kid], 0.0)
        out[256:288, :] = level1[pl.ds(which, 32, stride=2), :]


def cross_kernel(ids, mine, theirs, packed, cross, root):
    core = ids[0]
    total = jnp.zeros((256, 128), f32)
    for z in range(8):
        own = mine[z]
        root[4 * z : 4 * z + 4, :] = jnp.concatenate(
            [squares(own[:, 128 * h : 128 * h + 128]) for h in range(4)], axis=0
        )
        high, low = split(jnp.concatenate([own, theirs[z]], axis=0))
        panel = jnp.concatenate(
            [packed[2 * z + h // 2, (h % 2) ^ core, 0:128, :] for h in range(4)], axis=0
        )
        panel_high, panel_low = split(panel)
        both = dot(high, jnp.concatenate([panel_high, panel_low], axis=1))
        total = total + (both[:, :128] + both[:, 128:]) + dot(low, panel_high)
    cross[...] = total


def child_kernel(
    ids, parents, widths, blocks, mine, theirs, packed, child_inv,
    image, below_high, below_low, base, spread_high, spread_low,
):
    core = ids[0]
    spread_high[...] = jnp.zeros_like(spread_high)
    spread_low[...] = jnp.zeros_like(spread_low)
    for place, kid in enumerate(kids_of(parents, core)):
        for s in range(64):
            row = pl.multiple_of(blocks[kid, s] * BLOCK_ROWS, BLOCK_ROWS)
            start = 128 + 64 * place + 32 * (s % 2)
            piece = packed[s // 4, ((s // 2) % 2) ^ core, start : start + 32, :]
            high, low = split(piece)
            spread_high[pl.ds(row, 32), 128 * place : 128 * place + 128] = high
            spread_low[pl.ds(row, 32), 128 * place : 128 * place + 128] = low
    total = jnp.zeros((256, 256), f32)
    for z in range(8):
        high, low = split(jnp.concatenate([mine[z], theirs[z]], axis=0))
        up = spread_high[512 * z : 512 * z + 512, :]
        down = spread_low[512 * z : 512 * z + 512, :]
        total = total + dot(high, up) + dot(high, down) + dot(low, up)
    image[...] = total
    below_high[...] = spread_high[4096:5120, :]
    below_low[...] = spread_low[4096:5120, :]
    rows = ids[2] * 32 + lax.broadcasted_iota(jnp.int32, (32, 128), 0)
    lanes = ids[1] * 128 + lax.broadcasted_iota(jnp.int32, (32, 128), 1)
    for j in range(4):
        live = jnp.logical_and(rows < widths[j], lanes < widths[j])
        base[j : j + 1, :] = squares(jnp.where(live, child_inv[j], 0.0))


def finish_kernel(
    ids, parents, image, below_high, below_low, cross, level1, root, base, payload,
):
    core = ids[0]
    total = image[...]
    lower = jnp.zeros((64, 256), f32)
    sums = []
    for z in range(8):
        up = below_high[128 * z : 128 * z + 128, :]
        down = below_low[128 * z : 128 * z + 128, :]
        high, low = split(cross[z])
        total = total - (dot(high, up) + dot(high, down) + dot(low, up))
        factor = level1[z]
        high, low = split(factor)
        lower = lower + dot(high, up) + dot(high, down) + dot(low, up)
        sums.append(squares(cross[z]) + squares(factor))
    child = squares(total) + squares(lower)
    first, second = kids_of(parents, core)
    place = lax.broadcasted_iota(jnp.int32, (4, 128), 0)
    ends = (
        base[...]
        + jnp.where(place == first, child[:, :128], 0.0)
        + jnp.where(place == second, child[:, 128:], 0.0)
    )
    for i in range(32):
        line = sums[i // 4]
        payload[i, 0:4, :] = ends
        payload[i, 4:5, :] = root[i : i + 1, :]
        payload[i, 5:6, :] = jnp.where(core == 0, line, 0.0)
        payload[i, 6:7, :] = jnp.where(core == 0, 0.0, line)
        payload[i, 7:8, :] = jnp.zeros((1, 128), f32)


def body(
    root_inv,
    level1_inv,
    level1_panel,
    child_inv,
    child_panel,
    child_width,
    child_parent,
    child_blocks,
):
    row = lax.axis_index("row")
    col = lax.axis_index("col")
    ids = jnp.stack([row % 2, col, row]).astype(jnp.int32)

    mine = lax.all_gather(root_inv, "col")
    keep, give = call(
        pack_kernel, [((288, 128), f32)] * 2, [SMEM] * 3 + [VMEM] * 3, 0, 600000
    )(
        ids, child_parent, child_width,
        level1_panel.reshape(256, 128), level1_inv.reshape(64, 128), child_panel,
    )
    got = lax.ppermute(give, "row", PAIRS)
    pair = jnp.stack([keep, got])
    packed = lax.all_gather(pair[:, :256], "row", axis_index_groups=SAME_CORE)
    level1 = lax.all_gather(pair[:, 256:].reshape(64, 128), "col")
    theirs = lax.ppermute(mine, "row", PAIRS)

    cross_part, root = call(
        cross_kernel, [((256, 128), f32), ((32, 128), f32)], [SMEM] + [VMEM] * 3,
        800_000_000, 8_000_000,
    )(ids, mine, theirs, packed)
    cross = lax.all_gather(cross_part, "col")

    image, below_high, below_low, base = call(
        child_kernel,
        [((256, 256), f32), ((1024, 256), bf16), ((1024, 256), bf16), ((4, 128), f32)],
        [SMEM] * 4 + [VMEM] * 4, 1_600_000_000, 10_000_000,
        [pltpu.VMEM((5120, 256), bf16), pltpu.VMEM((5120, 256), bf16)],
    )(ids, child_parent, child_width, child_blocks, mine, theirs, packed, child_inv)

    (payload,) = call(
        finish_kernel, [((32, 8, 128), f32)], [SMEM] * 2 + [VMEM] * 7,
        500_000_000, 3_000_000,
    )(ids, child_parent, image, below_high, below_low, cross, level1, root, base)
    total = jnp.sum(lax.all_to_all(payload, "row", 0, 0, tiled=True), axis=0)
    parent = lax.dynamic_slice(total[5:7], (0, 32 * (row % 4)), (2, 32))
    return total[4], parent, total[0:4]


def solution(mesh):
    placed = (
        P("row", "col"),
        P("row", None, "col"),
        P("row", None, "col"),
        P(None, "row", "col"),
        P(None, "row", "col"),
        P(),
        P(),
        P(),
    )
    return jax.shard_map(
        body,
        mesh=mesh,
        in_specs=placed,
        out_specs=(P("row"), P(None, "row"), P(None, "col")),
        check_vma=False,
    )
```

time: 1060 us -> 187 us (0.18)
  waiting for transfers between devices: 771 us -> 104 us
  blocking collectives: 106 us -> 20.7 us
  local copies, waits for them, and re-layouts: 83.2 us -> 14.7 us
  matrix products: 44.8 us -> 0 us
  other arithmetic: 21.2 us -> 0.85 us
  Pallas kernels: 0 us -> 12.1 us
    reduce_scatter x7 -> x0, waiting for transfers between devices: 596 us -> none  [the longest x4 324 us: body(): lax.psum_scatter(inner_rows(picked, owned_rows), 'row', scatter_dimension...]
    all_gather x7 -> x3, waiting for transfers between devices: 173 us -> 91 us  [the longest x1 51.5 us: body(): packed = lax.all_gather(pair[:, :256], 'row', axis_index_groups=SAME_CORE)]
    psum x1 -> x0, blocking collectives: 64.9 us -> none  [body(): leverage_child = lax.psum(jnp.stack(partials), 'row')]
    gather x7 -> x0, local copies, waits for them, and re-layouts: 45.6 us -> none  [the longest x4 42.4 us: body(): picked = jnp.take(ancestor, slots, axis=1)]
    dot_general x12 -> x0, matrix products: 44.8 us -> none  [the longest x6 33.4 us: inner_rows(): lax.dot_general(former, latter, (((0,), (0,)), ((), ())), precision=highe...]
    all_gather x2 -> x1, blocking collectives: 41.4 us -> 20.7 us  [body(): level1 = lax.all_gather(pair[:, 256:].reshape(64, 128), 'col')]
    concatenate x4 -> x0, local copies, waits for them, and re-layouts: 20.1 us -> none  [body(): jnp.concatenate([jnp.concatenate([root_cov, -cross_mine], axis=1), jnp.co...]
    unnamed x55 -> x34, local copies, waits for them, and re-layouts: 0.12 us -> 12.9 us
  transfers between devices with their start and end apart: 15 -> 6, of which waited for: 14 -> 6; matrix products, arithmetic and copies ran while one was open for 12% -> 0% of each run, Pallas kernels for 0% -> 3%
where the time goes in v1:
time: 187 us
  waiting for transfers between devices  104 us (56%)
  blocking collectives  20.7 us (11%)
  starting transfers between devices  20.4 us (11%)
  local copies, waits for them, and re-layouts  14.7 us (8%)
  between operations  13.9 us (7%)
  Pallas kernels  12.1 us (6%)
    all_gather x1, waiting for transfers between devices, body(): packed = lax.all_gather(pair[:, :256], 'row', axis_index_groups=SAME_CORE)  51.5 us
    all_gather x1, waiting for transfers between devices, body(): mine = lax.all_gather(root_inv, 'col')  33.4 us
    all_gather x1, blocking collectives, body(): level1 = lax.all_gather(pair[:, 256:].reshape(64, 128), 'col')  20.7 us
    unnamed x34, local copies, waits for them, and re-layouts  12.9 us
    all_to_all x1, starting transfers between devices, body(): total = jnp.sum(lax.all_to_all(payload, 'row', 0, 0, tiled=True), axis=0)  12.6 us
    all_to_all x1, waiting for transfers between devices, body(): total = jnp.sum(lax.all_to_all(payload, 'row', 0, 0, tiled=True), axis=0)  7.61 us
    all_gather x1, waiting for transfers between devices, body(): cross = lax.all_gather(cross_part, 'col')  6.13 us
    pallas_call x1, Pallas kernels, body(): call(child_kernel, [((256, 256), f32), ((1024, 256), bf16), ((1024, 256),...  4.75 us
  transfers between devices with their start and end apart: 6, of which 6 were waited for; matrix products, arithmetic and copies ran while one was open for 0% of the time, Pallas kernels for 3%

profile of v1, /device:TPU:1, one launch (start us, length us, event | category | flops | bytes accessed | tf_op | source)
XLA Modules:
  0.0 186.9 jit_solution(9463402652193127131)
XLA Ops:
  8.0 0.9 copy-done.8
  8.9 0.9 copy-done.9
  9.8 0.8 copy-done.11
  12.5 3.3 %collective-permute-start.1 = (f32[288,128]{1,0:T(8,128)S(1)}, f32[288,128]{1,0:T(8,128)S(1)}, u32[]{:S(2)}, u32[]{:S(2)}) collective-permute-start(f32[288,128]{1,0:T(8,128)S(1)} %get-tuple-element.12), channel_id=1, source_target_pairs={{0,8},{8,0},{16,24},{24,16},{32,40},{40,32},{48,56},{56,48},{64,72... | collective-permute-start | bytes 442376 | tf_op jit(solution)/shard_map/ppermute | solution.py:164
  15.8 1.0 collective-permute-done.1
  16.8 0.7 fusion
  17.6 33.4 %all-gather.7.cloned.1.call-done = f32[1024,512]{1,0:T(8,128)} async-done(((f32[128,512]{1,0:T(8,128)}), f32[1024,512]{1,0:T(8,128)}) %all-gather.7.cloned.1.call-update) | async-done | bytes 2097168 | tf_op jit(solution)/shard_map/all_gather | solution.py:157
  51.0 4.4 %collective-permute-start = (f32[8,128,512]{2,1,0:T(8,128)}, f32[8,128,512]{2,1,0:T(8,128)S(1)}, u32[]{:S(2)}, u32[]{:S(2)}) collective-permute-start(f32[8,128,512]{2,1,0:T(8,128)} %bitcast.13), channel_id=1, source_target_pairs={{0,8},{8,0},{16,24},{24,16},{32,40},{40,32},{48,56},{56,48},{64,72... | collective-permute-start | bytes 6291464 | tf_op jit(solution)/shard_map/ppermute | solution.py:168
  55.4 4.0 %collective-permute-done.theirs = f32[8,128,512]{2,1,0:T(8,128)S(1)} collective-permute-done((f32[8,128,512]{2,1,0:T(8,128)}, f32[8,128,512]{2,1,0:T(8,128)S(1)}, u32[]{:S(2)}, u32[]{:S(2)}) %collective-permute-start) | collective-permute-done | bytes 2097184 | tf_op jit(solution)/shard_map/ppermute | solution.py:168
  59.4 1.4 copy-done.2
  60.8 51.5 %all-gather.9.cloned.1.call-done = f32[32,256,128]{2,1,0:T(8,128)} async-done(((f32[2,256,128]{2,1,0:T(8,128)}), f32[32,256,128]{2,1,0:T(8,128)}) %all-gather.9.cloned.1.call-update) | async-done | bytes 4194320 | tf_op jit(solution)/shard_map/all_gather | solution.py:166
  112.3 1.6 copy-done
  113.9 1.6 copy-done.3
  115.5 4.4 %shard_map.105 = (f32[256,128]{1,0:T(8,128)}, f32[32,128]{1,0:T(8,128)S(1)}) custom-call(s32[3]{0:T(128)S(1)} %pad_add_fusion.ids, f32[8,128,512]{2,1,0:T(8,128)S(1)} %bitcast.14, f32[8,128,512]{2,1,0:T(8,128)S(1)} %copy-done.3, f32[16,2,256,128]{3,2,1,0:T(8,128)} %bitcast.21), custom_call_target="tpu_custom_call" | custom-call | flops 800000000 | bytes 8000000 | tf_op jit(solution)/shard_map/pallas_call | solution.py:170
  119.9 20.7 %all_gather.27.level1 = f32[8,64,128]{2,1,0:T(8,128)S(1)} all-gather(f32[1,64,128]{2,1,0:T(8,128)S(1)} %bitcast.25), channel_id=1, replica_groups=mesh['row'=32,'col'=8] {'col'}, dimensions={0}, use_global_device_ids=true | all-gather | bytes 294912 | tf_op jit(solution)/shard_map/all_gather | solution.py:167
  140.6 1.6 copy-done.4
  142.2 4.7 %shard_map.104 = (f32[256,256]{1,0:T(8,128)S(1)}, bf16[1024,256]{1,0:T(8,128)(2,1)S(1)}, bf16[1024,256]{1,0:T(8,128)(2,1)S(1)}, f32[4,128]{1,0:T(4,128)S(1)}) custom-call(s32[3]{0:T(128)S(1)} %pad_add_fusion.ids, s32[4]{0:T(128)S(1)} %copy-done.13, s32[4]{0:T(128)S(1)} %copy-done.16, s32[4,64]{1,0:T(4,128)S(1)} %copy-done.14, f32[8,128,512]{2,1,0:T(8,128)S(1)} %bitcast.15, ...), custom_call_target="tpu_custom_call" | custom-call | flops 1600000000 | bytes 10000000 | tf_op jit(solution)/shard_map/pallas_call | solution.py:176
  147.0 0.7 copy-done.6
  147.7 6.1 %all-gather.11.cloned.1.call-done = f32[2048,128]{1,0:T(8,128)} async-done(((f32[256,128]{1,0:T(8,128)}), f32[2048,128]{1,0:T(8,128)}) %all-gather.11.cloned.1.call-update) | async-done | bytes 1048592 | tf_op jit(solution)/shard_map/all_gather | solution.py:174
  153.8 1.2 copy-done.5
  155.0 0.9 copy-done.7
  156.0 2.4 %shard_map.106 = f32[32,8,128]{2,1,0:T(8,128)} custom-call(s32[3]{0:T(128)S(1)} %pad_add_fusion.ids, s32[4]{0:T(128)S(1)} %copy-done.13, f32[256,256]{1,0:T(8,128)S(1)} %copy-done.7, bf16[1024,256]{1,0:T(8,128)(2,1)S(1)} %get-tuple-element.14.below_high, bf16[1024,256]{1,0:T(8,128)(2,1)S(1)} %get-tuple-element.15.below_low, f32[8,256,128]{2,1,0:T(8,128)S(1)} %bitcast.16, ...), custom_call_target="tpu_custom_call" | custom-call | flops 500000000 | bytes 3000000 | tf_op jit(solution)/shard_map/pallas_call | solution.py:183
  158.4 12.6 %all-to-all-start = ((f32[32,8,128]{2,1,0:T(8,128)}), f32[32,8,128]{2,1,0:T(8,128)S(1)}, u32[]{:S(2)}, u32[]{:S(2)}) async-start(f32[32,8,128]{2,1,0:T(8,128)} %shard_map.106), calls=%async_computation | async-start | bytes 262144 | tf_op jit(solution)/shard_map/all_to_all | solution.py:187
  171.0 7.6 %all-to-all-done = f32[32,8,128]{2,1,0:T(8,128)S(1)} async-done(((f32[32,8,128]{2,1,0:T(8,128)}), f32[32,8,128]{2,1,0:T(8,128)S(1)}, u32[]{:S(2)}, u32[]{:S(2)}) %all-to-all-start) | async-done | bytes 131104 | tf_op jit(solution)/shard_map/all_to_all | solution.py:187
  (38 shorter events, 4.6 us)
Async XLA Ops:
  7.2 43.9 %all-gather.7.cloned.1.call-start = ((), (), s32[]{:S(2)}) async-start(), calls=%async_computation.1 | async-start | bytes 2359296 | tf_op jit(solution)/shard_map/all_gather | solution.py:157
  7.9 104.4 %all-gather.9.cloned.1.call-start = ((), (), s32[]{:S(2)}) async-start(), calls=%async_computation.2 | async-start | bytes 4456448 | tf_op jit(solution)/shard_map/all_gather | solution.py:166
  8.0 0.9 copy-start.8
  8.9 0.9 copy-start.9
  9.8 0.8 copy-start.11
  10.6 0.7 copy-start.12
  11.3 0.7 copy-start.15
  12.5 4.3 %collective-permute-start.1 = (f32[288,128]{1,0:T(8,128)S(1)}, f32[288,128]{1,0:T(8,128)S(1)}, u32[]{:S(2)}, u32[]{:S(2)}) collective-permute-start(f32[288,128]{1,0:T(8,128)S(1)} %get-tuple-element.12), channel_id=1, source_target_pairs={{0,8},{8,0},{16,24},{24,16},{32,40},{40,32},{48,56},{56,48},{64,72... | collective-permute-start | bytes 442376 | tf_op jit(solution)/shard_map/ppermute | solution.py:164
  17.6 136.2 %all-gather.11.cloned.1.call-start = ((), (), s32[]{:S(2)}) async-start(), calls=%async_computation.3 | async-start | bytes 1179648 | tf_op jit(solution)/shard_map/all_gather | solution.py:174
  51.0 8.4 %collective-permute-start = (f32[8,128,512]{2,1,0:T(8,128)}, f32[8,128,512]{2,1,0:T(8,128)S(1)}, u32[]{:S(2)}, u32[]{:S(2)}) collective-permute-start(f32[8,128,512]{2,1,0:T(8,128)} %bitcast.13), channel_id=1, source_target_pairs={{0,8},{8,0},{16,24},{24,16},{32,40},{40,32},{48,56},{56,48},{64,72... | collective-permute-start | bytes 6291464 | tf_op jit(solution)/shard_map/ppermute | solution.py:168
  59.4 1.4 copy-start.2
  112.3 1.6 copy-start
  113.9 1.6 copy-start.3
  115.5 25.1 %copy-start.1 = (f32[1024,512]{1,0:T(8,128)S(1)}, f32[1024,512]{1,0:T(8,128)}, u32[]{:S(2)}) copy-start(f32[1024,512]{1,0:T(8,128)} %all-gather.7.cloned.1.call-done) | copy-start | bytes 6291460
  115.5 25.1 %copy-start.10 = (f32[4,32,128]{2,1,0:T(8,128)S(1)}, f32[4,32,128]{2,1,0:T(8,128)}, u32[]{:S(2)}) copy-start(f32[4,32,128]{2,1,0:T(8,128)} %child_inv.1) | copy-start | bytes 196612
  115.5 25.1 %copy-start.13 = (s32[4]{0:T(128)S(1)}, s32[4]{0:T(128)}, u32[]{:S(2)}) copy-start(s32[4]{0:T(128)} %parents.5) | copy-start | bytes 52
  115.5 25.1 %copy-start.14 = (s32[4,64]{1,0:T(4,128)S(1)}, s32[4,64]{1,0:T(4,128)}, u32[]{:S(2)}) copy-start(s32[4,64]{1,0:T(4,128)} %blocks.1) | copy-start | bytes 3076
  115.5 25.1 %copy-start.16 = (s32[4]{0:T(128)S(1)}, s32[4]{0:T(128)}, u32[]{:S(2)}) copy-start(s32[4]{0:T(128)} %widths.3) | copy-start | bytes 52
  140.6 1.6 copy-start.4
  147.0 0.7 copy-start.6
  153.8 1.2 copy-start.5
  155.0 0.9 copy-start.7
  158.4 20.2 %all-to-all-start = ((f32[32,8,128]{2,1,0:T(8,128)}), f32[32,8,128]{2,1,0:T(8,128)S(1)}, u32[]{:S(2)}, u32[]{:S(2)}) async-start(f32[32,8,128]{2,1,0:T(8,128)} %shard_map.106), calls=%async_computation | async-start | bytes 262144 | tf_op jit(solution)/shard_map/all_to_all | solution.py:187
Sparse Core Ops, SparseCore 0:
  9.8 41.1 all-gather.6
  53.5 58.7 all-gather.8
  120.0 33.7 all-gather.10

commit v2 on v0

v2 whole, which is shorter than its diff:
```python
import jax
import jax.numpy as jnp
from jax import lax
from jax.experimental import pallas as pl
from jax.experimental.pallas import tpu as pltpu
from jax.sharding import PartitionSpec as P

BLOCK_ROWS = 32
PAIRS = [(i, i ^ 1) for i in range(32)]
f32 = jnp.float32
bf16 = jnp.bfloat16

VMEM = pl.BlockSpec(memory_space=pltpu.VMEM)
ANY = pl.BlockSpec(memory_space=pl.ANY)
HBM = pl.BlockSpec(memory_space=pltpu.HBM)
SMEM = pl.BlockSpec(memory_space=pltpu.SMEM)


def call(kernel, outs, ins, cost, scratch=(), mib=60):
    return pl.pallas_call(
        kernel,
        out_shape=[jax.ShapeDtypeStruct(*out) for out in outs],
        in_specs=ins,
        out_specs=[VMEM] * len(outs),
        scratch_shapes=list(scratch),
        compiler_params=pltpu.CompilerParams(vmem_limit_bytes=60 * 1024 * 1024),
        cost_estimate=pl.CostEstimate(flops=cost[0], bytes_accessed=cost[1], transcendentals=0),
    )


def split(x):
    high = x.astype(bf16)
    return high, (x - high.astype(f32)).astype(bf16)


def dot(a, b):
    return jnp.dot(a, b, preferred_element_type=f32)


def product(x, high, low):
    up, down = split(x)
    rows = x.shape[0]
    both = dot(jnp.concatenate([up, down], axis=0), high)
    return both[:rows] + both[rows:] + dot(up, low)


def squares(x):
    return jnp.sum(x * x, axis=0, keepdims=True)


def kids_in_order(parents):
    order = []
    for which in range(2):
        hit = [parents[j] == which for j in range(4)]
        order.append(jnp.where(hit[0], 0, jnp.where(hit[1], 1, 2)))
        order.append(jnp.where(hit[3], 3, jnp.where(hit[2], 2, 1)))
    return order


def pack_kernel(root_inv, level1, panel, out, apart):
    out[0:128, :] = root_inv[...]
    for which in range(2):
        apart[which] = panel[pl.ds(which, 128, stride=2), :]
    for q in range(4):
        out[128:144, 128 * q : 128 * q + 128] = level1[16 * q : 16 * q + 16, :]


def chip_of(ids):
    return ids[2] // 8, (ids[2] // 2) % 4


def fetch_plane(parts, into, arrived):
    copies = []
    for side in range(2):
        zero, one, three, low, high = parts[5 * side : 5 * side + 5]
        for part, far, steps in (
            (zero, 0, (0, 1, 2, 3)),
            (one, 1, (0, 1, 2, 3)),
            (three, 3, (0, 1, 2, 3)),
            (low, 2, (0, 1)),
            (high, 2, (2, 3)),
        ):
            spot = into.at[4 * side + far, pl.ds(steps[0], len(steps))]
            copy = pltpu.make_async_copy(part, spot, arrived.at[len(copies)])
            copies.append((copy, side, far, steps))
    return copies


def fetch_rows(rows, factor, arrived):
    return [
        pltpu.make_async_copy(rows.at[z, pl.ds(0, 128)], factor.at[z], arrived.at[z])
        for z in range(8)
    ]


def split_rows(copies, factor, both):
    for z, copy in enumerate(copies):
        copy.wait()
        high, low = split(factor[z])
        both[0:128, 512 * z : 512 * z + 512] = high
        both[128:256, 512 * z : 512 * z + 512] = low


def times_rows(both, high, low):
    first = dot(both[...], high)
    return first[:128] + first[128:] + dot(both[0:128, :], low)


def cross_kernel(ids, rows, *refs):
    parts, refs = refs[:10], refs[10:]
    cross, root, factor, panels, both, high, low, row_here, panel_here = refs
    row_copies = fetch_rows(rows, factor, row_here)
    copies = fetch_plane(parts, panels, panel_here)
    for copy in row_copies + [c[0] for c in copies]:
        copy.start()
    split_rows(row_copies, factor, both)
    for z in range(8):
        root[z] = squares(factor[z])
    chip_y, chip_x = chip_of(ids)
    for copy, side, far, steps in copies:
        copy.wait()
        core = ids[0] if side == 0 else 1 - ids[0]
        for step in steps:
            chip = (chip_y + 4 - step) % 4 * 4 + (chip_x + 4 - far) % 4
            spot = pl.ds(pl.multiple_of(128 * (2 * chip + core), 128), 128)
            for which in range(2):
                up, down = split(panels[4 * side + far, step, which])
                high[spot, 128 * which : 128 * which + 128] = up
                low[spot, 128 * which : 128 * which + 128] = down
    cross[...] = times_rows(both, high[...], low[...])


def child_kernel(ids, parents, widths, blocks, rows, child_inv, *refs):
    parts, refs = refs[:10], refs[10:]
    image, below_high, below_low, base, lines = refs[:5]
    factor, level1, panels, both, high, low, row_here, part_here, tail_here = refs[5:]
    copies = fetch_plane(parts, panels, part_here)
    row_copies = fetch_rows(rows, factor, row_here)
    tail = pltpu.make_async_copy(rows.at[:, pl.ds(128, 16)], level1, tail_here)
    for copy in [c[0] for c in copies] + row_copies + [tail]:
        copy.start()
    high[...] = jnp.zeros_like(high)
    low[...] = jnp.zeros_like(low)
    chip_y, chip_x = chip_of(ids)
    lanes = ids[1] * 128 + lax.broadcasted_iota(jnp.int32, (32, 128), 1)
    order = kids_in_order(parents)
    live = [lanes < widths[kid] for kid in order]
    for copy, side, far, steps in copies:
        copy.wait()
        core = ids[0] if side == 0 else 1 - ids[0]
        for step in steps:
            chip = (chip_y + 4 - far) % 4 * 4 + (chip_x + 4 - step) % 4
            for half in range(2):
                slot = 4 * chip + 2 * core + half
                for place, kid in enumerate(order):
                    row = pl.multiple_of(blocks[kid, slot] * BLOCK_ROWS, BLOCK_ROWS)
                    piece = panels[4 * side + far, step, kid, 32 * half : 32 * half + 32, :]
                    up, down = split(jnp.where(live[place], piece, 0.0))
                    high[pl.ds(row, 32), 128 * place : 128 * place + 128] = up
                    low[pl.ds(row, 32), 128 * place : 128 * place + 128] = down
    split_rows(row_copies, factor, both)
    image[...] = times_rows(both, high[0:4096, :], low[0:4096, :])
    below_high[...] = high[4096:5120, :]
    below_low[...] = low[4096:5120, :]

    depth = ids[2] * 32 + lax.broadcasted_iota(jnp.int32, (32, 128), 0)
    for j in range(4):
        inside = jnp.logical_and(depth < widths[j], lanes < widths[j])
        base[j : j + 1, :] = squares(jnp.where(inside, child_inv[j], 0.0))
    tail.wait()
    own = jnp.concatenate(
        [
            jnp.concatenate([level1[n, :, 128 * q : 128 * q + 128] for n in range(8)], axis=1)
            for q in range(4)
        ],
        axis=0,
    )
    lower = product(own, high[4096:5120, :], low[4096:5120, :])
    parity = lax.broadcasted_iota(jnp.int32, (64, 1024), 0) % 2
    parity_half = lax.broadcasted_iota(jnp.int32, (64, 256), 0) % 2
    for which in range(2):
        half = slice(256 * which, 256 * which + 256)
        sums = squares(jnp.where(parity_half == which, lower[:, half], 0.0))
        base[...] += by_child(parents, which, sums)
        lines[which : which + 1, :] = squares(jnp.where(parity == which, own, 0.0))


def by_child(parents, which, sums):
    place = lax.broadcasted_iota(jnp.int32, (4, 128), 0)
    first, second = kids_in_order(parents)[2 * which : 2 * which + 2]
    return jnp.where(place == first, sums[:, :128], 0.0) + jnp.where(
        place == second, sums[:, 128:], 0.0
    )


def finish_kernel(ids, parents, root, base, lines, image, below_high, below_low, *refs):
    parts, (payload, cross, arrived) = refs[:9], refs[9:]
    copies = []
    for n, part in enumerate(parts):
        away = (0, 1, -1, 2, -2, 3, -3, 4, 4)[n]
        spot = cross.at[(ids[1] + 8 - away) % 8]
        if n >= 7:
            spot = spot.at[pl.ds(64 * (n - 7), 64)]
        copies.append(pltpu.make_async_copy(part, spot, arrived.at[n]))
    for copy in copies:
        copy.start()
    for copy in copies:
        copy.wait()
    ends = base[...]
    known_lines = []
    for which in range(2):
        half = slice(256 * which, 256 * which + 256)
        known = jnp.concatenate(
            [cross[z, :, 128 * which : 128 * which + 128] for z in range(8)], axis=1
        )
        upper = image[:, half] - product(known, below_high[:, half], below_low[:, half])
        ends = ends + by_child(parents, which, squares(upper))
        known_lines.append(lines[which : which + 1, :] + squares(known))
    for i in range(32):
        b = i // 4
        payload[i, 0:4, :] = ends
        payload[i, 4:5, :] = root[b, :, 128 * (i % 4) : 128 * (i % 4) + 128]
        payload[i, 5:6, :] = known_lines[0][:, 128 * b : 128 * b + 128]
        payload[i, 6:7, :] = known_lines[1][:, 128 * b : 128 * b + 128]
        payload[i, 7:8, :] = jnp.zeros((1, 128), f32)


def sum_kernel(ids, parts, root, parent, child):
    total = parts[0]
    for i in range(1, 32):
        total = total + parts[i]
    child[...] = total[0:4, :]
    root[...] = total[4:5, :]
    place = ids[2] % 4
    found = total[5:7, 0:32]
    for n in range(1, 4):
        found = jnp.where(place == n, total[5:7, 32 * n : 32 * n + 32], found)
    parent[...] = found


def moved(x, down, right):
    def target(i):
        y, x, core = i // 8, i // 2 % 4, i % 2
        return ((y + down) % 4 * 4 + (x + right) % 4) * 2 + core

    return lax.ppermute(x, "row", [(i, target(i)) for i in range(32)])


def around(x, step):
    one, three = step(x, 1), step(x, 3)
    return [x, one, three, step(one[:2], 1), step(three[2:], 3)]


def along(x, meanwhile):
    def moved(part, n):
        return lax.ppermute(part, "col", [(z, (z + n) % 8) for z in range(8)])

    first, meanwhile = lax.optimization_barrier(
        ([moved(x, n) for n in (1, -1, 2, -2)], meanwhile)
    )
    below, above = first[2:]
    second = [moved(below, 1), moved(above, -1), moved(below[:64], 2), moved(above[64:], -2)]
    return [x] + first + second, meanwhile


def body(
    root_inv,
    level1_inv,
    level1_panel,
    child_inv,
    child_panel,
    child_width,
    child_parent,
    child_blocks,
):
    row = lax.axis_index("row")
    col = lax.axis_index("col")
    ids = jnp.stack([row & 1, col, row]).astype(jnp.int32)

    packed, panel = call(
        pack_kernel, [((144, 512), f32), ((2, 128, 128), f32)], [VMEM] * 3, (0, 900_000)
    )(root_inv, level1_inv.reshape(64, 128), level1_panel.reshape(256, 128))
    rows = lax.all_gather(packed, "col")

    panels = jnp.stack([panel] + [moved(panel, n, 0) for n in (1, 2, 3)])
    children = jnp.stack([child_panel] + [moved(child_panel, 0, n) for n in (1, 2, 3)])
    panels = around(panels, lambda x, n: moved(x, 0, n))
    children = around(children, lambda x, n: moved(x, n, 0))
    panels = panels + [lax.ppermute(part, "row", PAIRS) for part in panels]
    panels, children = lax.optimization_barrier((panels, children))
    children = children + [lax.ppermute(part, "row", PAIRS) for part in children]

    cross, root = call(
        cross_kernel, [((128, 256), f32), ((8, 1, 512), f32)],
        [SMEM] + [HBM] * 11, (800_000_000, 6_000_000),
        [
            pltpu.VMEM((8, 128, 512), f32),
            pltpu.VMEM((8, 4, 2, 128, 128), f32),
            pltpu.VMEM((256, 4096), bf16),
            pltpu.VMEM((4096, 256), bf16),
            pltpu.VMEM((4096, 256), bf16),
            pltpu.SemaphoreType.DMA((8,)),
            pltpu.SemaphoreType.DMA((10,)),
        ],
    )(ids, rows, *panels)
    cross, children = lax.optimization_barrier((cross, children))

    worked = call(
        child_kernel,
        [
            ((128, 512), f32), ((1024, 512), bf16), ((1024, 512), bf16),
            ((4, 128), f32), ((2, 1024), f32),
        ],
        [SMEM] * 4 + [HBM, VMEM] + [HBM] * 10, (1_600_000_000, 10_000_000),
        [
            pltpu.VMEM((8, 128, 512), f32),
            pltpu.VMEM((8, 16, 512), f32),
            pltpu.VMEM((8, 4, 4, 64, 128), f32),
            pltpu.VMEM((256, 4096), bf16),
            pltpu.VMEM((5120, 512), bf16),
            pltpu.VMEM((5120, 512), bf16),
            pltpu.SemaphoreType.DMA((8,)),
            pltpu.SemaphoreType.DMA((10,)),
            pltpu.SemaphoreType.DMA,
        ],
        40,
    )(ids, child_parent, child_width, child_blocks, rows, child_inv, *children)
    crosses, (image, below_high, below_low, base, lines) = along(cross, worked)

    (payload,) = call(
        finish_kernel, [((32, 8, 128), f32)], [SMEM] * 2 + [VMEM] * 6 + [ANY] * 9,
        (500_000_000, 3_000_000),
        [pltpu.VMEM((8, 128, 256), f32), pltpu.SemaphoreType.DMA((9,))],
        16,
    )(ids, child_parent, root, base, lines, image, below_high, below_low, *crosses)
    root, parent, child = call(
        sum_kernel, [((1, 128), f32), ((2, 32), f32), ((4, 128), f32)], [SMEM, VMEM],
        (0, 130_000), (), 16,
    )(ids, lax.all_to_all(payload, "row", 0, 0, tiled=True))
    return root.reshape(128), parent, child


def solution(mesh):
    placed = (
        P("row", "col"),
        P("row", None, "col"),
        P("row", None, "col"),
        P(None, "row", "col"),
        P(None, "row", "col"),
        P(),
        P(),
        P(),
    )
    return jax.shard_map(
        body,
        mesh=mesh,
        in_specs=placed,
        out_specs=(P("row"), P(None, "row"), P(None, "col")),
        check_vma=False,
    )
```

time: 1060 us -> 121 us (0.11)
  waiting for transfers between devices: 771 us -> 21.2 us
  blocking collectives: 106 us -> 15.1 us
  local copies, waits for them, and re-layouts: 83.2 us -> 0.81 us
  matrix products: 44.8 us -> 0 us
  starting transfers between devices: 12 us -> 45.6 us
  Pallas kernels: 0 us -> 21.4 us
  other arithmetic: 21.2 us -> 2.54 us
    reduce_scatter x7 -> x0, waiting for transfers between devices: 596 us -> none  [the longest x4 324 us: body(): lax.psum_scatter(inner_rows(picked, owned_rows), 'row', scatter_dimension...]
    all_gather x7 -> x1, waiting for transfers between devices: 173 us -> 0.01 us  [body(): rows = lax.all_gather(packed, 'col')]
    psum x1 -> x0, blocking collectives: 64.9 us -> none  [body(): leverage_child = lax.psum(jnp.stack(partials), 'row')]
    gather x7 -> x0, local copies, waits for them, and re-layouts: 45.6 us -> none  [the longest x4 42.4 us: body(): picked = jnp.take(ancestor, slots, axis=1)]
    ppermute x0 -> x32, starting transfers between devices: none -> 45.6 us  [the longest x14 20.3 us: moved(): return lax.ppermute(x, 'row', [(i, target(i)) for i in range(32)])]
    dot_general x12 -> x0, matrix products: 44.8 us -> none  [the longest x6 33.4 us: inner_rows(): lax.dot_general(former, latter, (((0,), (0,)), ((), ())), precision=highe...]
    all_gather x2 -> x0, blocking collectives: 41.4 us -> none  [the longest x1 21 us: body(): lax.all_gather(level1_inv, 'col', axis=2, tiled=True)]
    pallas_call x0 -> x5, Pallas kernels: none -> 21.4 us  [the longest x1 7.37 us: body(): call(child_kernel, [((128, 512), f32), ((1024, 512), bf16), ((1024, 512),...]
  transfers between devices with their start and end apart: 15 -> 33, of which waited for: 14 -> 10; matrix products, arithmetic and copies ran while one was open for 12% -> 2% of each run, Pallas kernels for 0% -> 11%
where the time goes in v2:
time: 121 us
  starting transfers between devices  45.6 us (38%)
  Pallas kernels  21.4 us (18%)
  waiting for transfers between devices  21.2 us (18%)
  blocking collectives  15.1 us (12%)
  between operations  14.4 us (12%)
  other arithmetic  2.54 us (2%)
    ppermute x14, starting transfers between devices, moved(): return lax.ppermute(x, 'row', [(i, target(i)) for i in range(32)])  20.3 us
    all_to_all x1, blocking collectives, body(): lax.all_to_all(payload, 'row', 0, 0, tiled=True)  15.1 us
    ppermute x14, waiting for transfers between devices, moved(): return lax.ppermute(x, 'row', [(i, target(i)) for i in range(32)])  14.4 us
    ppermute x8, starting transfers between devices, moved(): return lax.ppermute(part, 'col', [(z, (z + n) % 8) for z in range(8)])  14.3 us
    ppermute x5, starting transfers between devices, body(): panels = panels + [lax.ppermute(part, 'row', PAIRS) for part in panels]  9.19 us
    pallas_call x1, Pallas kernels, body(): call(child_kernel, [((128, 512), f32), ((1024, 512), bf16), ((1024, 512),...  7.37 us
    pallas_call x1, Pallas kernels, body(): call(cross_kernel, [((128, 256), f32), ((8, 1, 512), f32)], [SMEM] + [HBM...  6.1 us
    ppermute x8, waiting for transfers between devices, moved(): return lax.ppermute(part, 'col', [(z, (z + n) % 8) for z in range(8)])  5.67 us
  transfers between devices with their start and end apart: 33, of which 10 were waited for; matrix products, arithmetic and copies ran while one was open for 2% of the time, Pallas kernels for 11%

profile of v2, /device:TPU:1, one launch (start us, length us, event | category | flops | bytes accessed | tf_op | source)
XLA Modules:
  0.0 121.0 jit_solution(14562676373957782605)
XLA Ops:
  7.2 1.8 %shard_map.103 = (f32[144,512]{1,0:T(8,128)}, f32[2,128,128]{2,1,0:T(8,128)}) custom-call(f32[128,512]{1,0:T(8,128)} %root_inv.1, f32[64,128]{1,0:T(8,128)} %bitcast.26, f32[256,128]{1,0:T(8,128)} %bitcast.17), custom_call_target="tpu_custom_call" | custom-call | bytes 900000 | tf_op jit(solution)/shard_map/pallas_call | solution.py:280
  9.0 3.6 %collective-permute-start.2 = (f32[2,128,128]{2,1,0:T(8,128)}, f32[2,128,128]{2,1,0:T(8,128)S(1)}, u32[]{:S(2)}, u32[]{:S(2)}) collective-permute-start(f32[2,128,128]{2,1,0:T(8,128)} %get-tuple-element.51), channel_id=1, source_target_pairs={{0,192},{8,200},{16,208},{24,216},{32,224},{40,232},{48,240},{56,2... | collective-permute-start | bytes 393224 | tf_op jit(solution)/shard_map/ppermute | solution.py:246
  16.6 4.1 %collective-permute-start.13 = (f32[4,64,128]{2,1,0:T(8,128)}, f32[4,64,128]{2,1,0:T(8,128)S(1)}, u32[]{:S(2)}, u32[]{:S(2)}) collective-permute-start(f32[4,64,128]{2,1,0:T(8,128)} %param.12), channel_id=1, source_target_pairs={{0,32},{8,40},{16,48},{24,56},{32,0},{40,8},{48,16},{56,24},{64,96... | collective-permute-start | bytes 393224 | tf_op jit(solution)/shard_map/ppermute | solution.py:246
  20.7 1.8 %collective-permute-done = f32[2,128,128]{2,1,0:T(8,128)S(1)} collective-permute-done((f32[2,128,128]{2,1,0:T(8,128)}, f32[2,128,128]{2,1,0:T(8,128)S(1)}, u32[]{:S(2)}, u32[]{:S(2)}) %collective-permute-start) | collective-permute-done | bytes 131104 | tf_op jit(solution)/shard_map/ppermute | solution.py:246
  23.4 2.6 %collective-permute-start.4 = (f32[4,2,128,128]{3,2,1,0:T(8,128)S(1)}, f32[4,2,128,128]{3,2,1,0:T(8,128)S(1)}, u32[]{:S(2)}, u32[]{:S(2)}) collective-permute-start(f32[4,2,128,128]{3,2,1,0:T(8,128)S(1)} %pad_maximum_fusion.refs_0_), channel_id=1, source_target_pairs={{0,48},{8,56},{16,0},{24,8},{32,16},{40,24},{48,32},{56,40},{64,11... | collective-permute-start | bytes 1572872 | tf_op jit(solution)/shard_map/ppermute | solution.py:246
  27.8 3.5 %collective-permute-start.7 = (f32[4,2,128,128]{3,2,1,0:T(8,128)S(1)}, f32[4,2,128,128]{3,2,1,0:T(8,128)S(1)}, u32[]{:S(2)}, u32[]{:S(2)}) collective-permute-start(f32[4,2,128,128]{3,2,1,0:T(8,128)S(1)} %pad_maximum_fusion.refs_0_), channel_id=1, source_target_pairs={{0,8},{8,0},{16,24},{24,16},{32,40},{40,32},{48,56},{56,48},{64,72... | collective-permute-start | bytes 1572872 | tf_op jit(solution)/shard_map/ppermute | solution.py:289
  31.3 5.4 %collective-permute-done.4.refs_2_ = f32[4,2,128,128]{3,2,1,0:T(8,128)S(1)} collective-permute-done((f32[4,2,128,128]{3,2,1,0:T(8,128)S(1)}, f32[4,2,128,128]{3,2,1,0:T(8,128)S(1)}, u32[]{:S(2)}, u32[]{:S(2)}) %collective-permute-start.4) | collective-permute-done | bytes 524320 | tf_op jit(solution)/shard_map/ppermute | solution.py:246
  36.7 3.6 %collective-permute-start.6 = (f32[2,2,128,128]{3,2,1,0:T(8,128)S(1)}, f32[2,2,128,128]{3,2,1,0:T(8,128)S(1)}, u32[]{:S(2)}, u32[]{:S(2)}) collective-permute-start(f32[2,2,128,128]{3,2,1,0:T(8,128)S(1)} %slice.25), channel_id=1, source_target_pairs={{0,48},{8,56},{16,0},{24,8},{32,16},{40,24},{48,32},{56,40},{64,11... | collective-permute-start | bytes 786440 | tf_op jit(solution)/shard_map/ppermute | solution.py:246
  40.4 1.7 %collective-permute-start.9 = (f32[4,2,128,128]{3,2,1,0:T(8,128)S(1)}, f32[4,2,128,128]{3,2,1,0:T(8,128)S(1)}, u32[]{:S(2)}, u32[]{:S(2)}) collective-permute-start(f32[4,2,128,128]{3,2,1,0:T(8,128)S(1)} %collective-permute-done.4.refs_2_), channel_id=1, source_target_pairs={{0,8},{8,0},{16,24},{24,16},{32,40},{40,32},{48,56},{56,48},{64,72... | collective-permute-start | bytes 1572872 | tf_op jit(solution)/shard_map/ppermute | solution.py:289
  42.3 3.9 %collective-permute-done.15.refs_1_ = f32[4,4,64,128]{3,2,1,0:T(8,128)S(1)} collective-permute-done((f32[4,4,64,128]{3,2,1,0:T(8,128)S(1)}, f32[4,4,64,128]{3,2,1,0:T(8,128)S(1)}, u32[]{:S(2)}, u32[]{:S(2)}) %collective-permute-start.15) | collective-permute-done | bytes 524320 | tf_op jit(solution)/shard_map/ppermute | solution.py:246
  46.2 1.7 %collective-permute-start.17 = (f32[2,4,64,128]{3,2,1,0:T(8,128)S(1)}, f32[2,4,64,128]{3,2,1,0:T(8,128)}, u32[]{:S(2)}, u32[]{:S(2)}) collective-permute-start(f32[2,4,64,128]{3,2,1,0:T(8,128)S(1)} %slice.26), channel_id=1, source_target_pairs={{0,64},{8,72},{16,80},{24,88},{32,96},{40,104},{48,112},{56,120},{... | collective-permute-start | bytes 786440 | tf_op jit(solution)/shard_map/ppermute | solution.py:246
  48.0 2.4 %collective-permute-start.11 = (f32[2,2,128,128]{3,2,1,0:T(8,128)S(1)}, f32[2,2,128,128]{3,2,1,0:T(8,128)S(1)}, u32[]{:S(2)}, u32[]{:S(2)}) collective-permute-start(f32[2,2,128,128]{3,2,1,0:T(8,128)S(1)} %collective-permute-done.6.refs_4_), channel_id=1, source_target_pairs={{0,8},{8,0},{16,24},{24,16},{32,40},{40,32},{48,56},{56,48},{64,72... | collective-permute-start | bytes 786440 | tf_op jit(solution)/shard_map/ppermute | solution.py:289
  50.3 3.1 %collective-permute-done.18.refs_4_ = f32[2,4,64,128]{3,2,1,0:T(8,128)S(1)} collective-permute-done((f32[2,4,64,128]{3,2,1,0:T(8,128)S(1)}, f32[2,4,64,128]{3,2,1,0:T(8,128)S(1)}, u32[]{:S(2)}, u32[]{:S(2)}) %collective-permute-start.18) | collective-permute-done | bytes 262176 | tf_op jit(solution)/shard_map/ppermute | solution.py:246
  58.6 6.1 %shard_map.104 = (f32[128,256]{1,0:T(8,128)}, f32[8,1,512]{2,1,0:T(1,128)}) custom-call(s32[3]{0:T(128)} %pad_add_fusion.ids, f32[8,144,512]{2,1,0:T(8,128)} %bitcast.15, f32[4,2,128,128]{3,2,1,0:T(8,128)} %copy-done.1, f32[4,2,128,128]{3,2,1,0:T(8,128)} %copy-done.5, f32[4,2,128,128]{3,2,1,0:T(8,128)} %copy-done.4, f32[2,2,128,128]{3,2,1,0:T(8,128)} %copy-done.13, ...), custom_call_target="tpu_custom_call" | custom-call | flops 800000000 | bytes 6000000 | tf_op jit(solution)/shard_map/pallas_call | solution.py:293
  64.7 6.0 %collective-permute-start.27 = (f32[128,256]{1,0:T(8,128)}, f32[128,256]{1,0:T(8,128)S(1)}, u32[]{:S(2)}, u32[]{:S(2)}) collective-permute-start(f32[128,256]{1,0:T(8,128)} %get-tuple-element.69.refs_0_), channel_id=1, source_target_pairs={{0,6},{1,7},{2,0},{3,1},{4,2},{5,3},{6,4},{7,5},{8,14},{9,15},{10,... | collective-permute-start | bytes 393224 | tf_op jit(solution)/shard_map/ppermute | solution.py:256
  70.8 3.2 %collective-permute-start.25 = (f32[128,256]{1,0:T(8,128)}, f32[128,256]{1,0:T(8,128)S(1)}, u32[]{:S(2)}, u32[]{:S(2)}) collective-permute-start(f32[128,256]{1,0:T(8,128)} %get-tuple-element.69.refs_0_), channel_id=1, source_target_pairs={{0,7},{1,0},{2,1},{3,2},{4,3},{5,4},{6,5},{7,6},{8,15},{9,8},{10,9... | collective-permute-start | bytes 393224 | tf_op jit(solution)/shard_map/ppermute | solution.py:256
  74.0 7.4 %shard_map.105 = (f32[128,512]{1,0:T(8,128)}, bf16[1024,512]{1,0:T(8,128)(2,1)}, bf16[1024,512]{1,0:T(8,128)(2,1)}, f32[4,128]{1,0:T(4,128)}, f32[2,1024]{1,0:T(2,128)}) custom-call(s32[3]{0:T(128)} %pad_add_fusion.ids, s32[4]{0:T(128)} %parents.3, s32[4]{0:T(128)} %widths.1, s32[4,64]{1,0:T(4,128)} %blocks.1, f32[8,144,512]{2,1,0:T(8,128)} %bitcast.16, ...), custom_call_target="tpu_custom_call" | custom-call | flops 1600000000 | bytes 10000000 | tf_op jit(solution)/shard_map/pallas_call | solution.py:308
  81.4 2.0 %collective-permute-done.24.refs_1_ = f32[128,256]{1,0:T(8,128)S(1)} collective-permute-done((f32[128,256]{1,0:T(8,128)}, f32[128,256]{1,0:T(8,128)S(1)}, u32[]{:S(2)}, u32[]{:S(2)}) %collective-permute-start.24) | collective-permute-done | bytes 131104 | tf_op jit(solution)/shard_map/ppermute | solution.py:256
  83.4 2.7 %collective-permute-start.29 = (f32[128,256]{1,0:T(8,128)S(1)}, f32[128,256]{1,0:T(8,128)S(1)}, u32[]{:S(2)}, u32[]{:S(2)}) collective-permute-start(f32[128,256]{1,0:T(8,128)S(1)} %collective-permute-done.27.refs_4_), channel_id=1, source_target_pairs={{0,7},{1,0},{2,1},{3,2},{4,3},{5,4},{6,5},{7,6},{8,15},{9,8},{10,9... | collective-permute-start | bytes 393224 | tf_op jit(solution)/shard_map/ppermute | solution.py:256
  86.2 2.4 %collective-permute-start.30 = (f32[64,256]{1,0:T(8,128)S(1)}, f32[64,256]{1,0:T(8,128)S(1)}, u32[]{:S(2)}, u32[]{:S(2)}) collective-permute-start(f32[64,256]{1,0:T(8,128)S(1)} %slice.22), channel_id=1, source_target_pairs={{0,2},{1,3},{2,4},{3,5},{4,6},{5,7},{6,0},{7,1},{8,10},{9,11},{10,... | collective-permute-start | bytes 196616 | tf_op jit(solution)/shard_map/ppermute | solution.py:256
  88.6 2.5 %collective-permute-done.31.refs_8_ = f32[64,256]{1,0:T(8,128)S(1)} collective-permute-done((f32[64,256]{1,0:T(8,128)S(1)}, f32[64,256]{1,0:T(8,128)S(1)}, u32[]{:S(2)}, u32[]{:S(2)}) %collective-permute-start.31) | collective-permute-done | bytes 65568 | tf_op jit(solution)/shard_map/ppermute | solution.py:256
  92.9 4.3 %shard_map.106 = f32[32,8,128]{2,1,0:T(8,128)} custom-call(s32[3]{0:T(128)} %pad_add_fusion.ids, s32[4]{0:T(128)} %parents.3, f32[8,1,512]{2,1,0:T(1,128)} %get-tuple-element.62.root, f32[4,128]{1,0:T(4,128)} %get-tuple-element.85.base, f32[2,1024]{1,0:T(2,128)} %get-tuple-element.86.lines, f32[128,512]{1,0:T(8,128)} %get-tuple-element.87.image, ...), custom_call_target="tpu_custom_call" | custom-call | flops 500000000 | bytes 3000000 | tf_op jit(solution)/shard_map/pallas_call | solution.py:330
  97.2 15.1 %all_to_all.5.parts = f32[32,8,128]{2,1,0:T(8,128)} all-to-all(f32[32,8,128]{2,1,0:T(8,128)} %shard_map.106), channel_id=1, replica_groups=mesh['row'=32,'col'=8] {'row'}, dimensions={0} | all-to-all | bytes 262144 | tf_op jit(solution)/shard_map/all_to_all | solution.py:339
  112.3 1.8 %shard_map.107 = (f32[1,128]{1,0:T(1,128)}, f32[2,32]{1,0:T(2,128)}, f32[4,128]{1,0:T(4,128)}) custom-call(s32[3]{0:T(128)} %pad_add_fusion.ids, f32[32,8,128]{2,1,0:T(8,128)} %all_to_all.5.parts), custom_call_target="tpu_custom_call" | custom-call | bytes 130000 | tf_op jit(solution)/shard_map/pallas_call | solution.py:336
  (102 shorter events, 14.0 us)
Async XLA Ops:
  7.2 51.4 %all-gather.3.cloned.1.call-start = ((), (), s32[]{:S(2)}) async-start(), calls=%async_computation.1 | async-start | bytes 2654208 | tf_op jit(solution)/shard_map/all_gather | solution.py:283
  12.7 8.1 %collective-permute-start.1 = (f32[2,128,128]{2,1,0:T(8,128)}, f32[2,128,128]{2,1,0:T(8,128)S(1)}, u32[]{:S(2)}, u32[]{:S(2)}) collective-permute-start(f32[2,128,128]{2,1,0:T(8,128)} %get-tuple-element.51), channel_id=1, source_target_pairs={{0,128},{8,136},{16,144},{24,152},{32,160},{40,168},{48,176},{56,1... | collective-permute-start | bytes 393224 | tf_op jit(solution)/shard_map/ppermute | solution.py:246
  13.0 9.5 %collective-permute-start = (f32[2,128,128]{2,1,0:T(8,128)}, f32[2,128,128]{2,1,0:T(8,128)S(1)}, u32[]{:S(2)}, u32[]{:S(2)}) collective-permute-start(f32[2,128,128]{2,1,0:T(8,128)} %get-tuple-element.51), channel_id=1, source_target_pairs={{0,64},{8,72},{16,80},{24,88},{32,96},{40,104},{48,112},{56,120},{... | collective-permute-start | bytes 393224 | tf_op jit(solution)/shard_map/ppermute | solution.py:246
  13.7 12.3 %collective-permute-start.12 = (f32[4,64,128]{2,1,0:T(8,128)}, f32[4,64,128]{2,1,0:T(8,128)S(1)}, u32[]{:S(2)}, u32[]{:S(2)}) collective-permute-start(f32[4,64,128]{2,1,0:T(8,128)} %param.12), channel_id=1, source_target_pairs={{0,16},{8,24},{16,32},{24,40},{32,48},{40,56},{48,0},{56,8},{64,80... | collective-permute-start | bytes 393224 | tf_op jit(solution)/shard_map/ppermute | solution.py:246
  14.9 11.1 %collective-permute-start.14 = (f32[4,64,128]{2,1,0:T(8,128)}, f32[4,64,128]{2,1,0:T(8,128)S(1)}, u32[]{:S(2)}, u32[]{:S(2)}) collective-permute-start(f32[4,64,128]{2,1,0:T(8,128)} %param.12), channel_id=1, source_target_pairs={{0,48},{8,56},{16,0},{24,8},{32,16},{40,24},{48,32},{56,40},{64,11... | collective-permute-start | bytes 393224 | tf_op jit(solution)/shard_map/ppermute | solution.py:246
  16.6 9.4 %collective-permute-start.13 = (f32[4,64,128]{2,1,0:T(8,128)}, f32[4,64,128]{2,1,0:T(8,128)S(1)}, u32[]{:S(2)}, u32[]{:S(2)}) collective-permute-start(f32[4,64,128]{2,1,0:T(8,128)} %param.12), channel_id=1, source_target_pairs={{0,32},{8,40},{16,48},{24,56},{32,0},{40,8},{48,16},{56,24},{64,96... | collective-permute-start | bytes 393224 | tf_op jit(solution)/shard_map/ppermute | solution.py:246
  23.4 13.2 %collective-permute-start.4 = (f32[4,2,128,128]{3,2,1,0:T(8,128)S(1)}, f32[4,2,128,128]{3,2,1,0:T(8,128)S(1)}, u32[]{:S(2)}, u32[]{:S(2)}) collective-permute-start(f32[4,2,128,128]{3,2,1,0:T(8,128)S(1)} %pad_maximum_fusion.refs_0_), channel_id=1, source_target_pairs={{0,48},{8,56},{16,0},{24,8},{32,16},{40,24},{48,32},{56,40},{64,11... | collective-permute-start | bytes 1572872 | tf_op jit(solution)/shard_map/ppermute | solution.py:246
  26.0 14.3 %collective-permute-start.3 = (f32[4,2,128,128]{3,2,1,0:T(8,128)S(1)}, f32[4,2,128,128]{3,2,1,0:T(8,128)S(1)}, u32[]{:S(2)}, u32[]{:S(2)}) collective-permute-start(f32[4,2,128,128]{3,2,1,0:T(8,128)S(1)} %pad_maximum_fusion.refs_0_), channel_id=1, source_target_pairs={{0,16},{8,24},{16,32},{24,40},{32,48},{40,56},{48,0},{56,8},{64,80... | collective-permute-start | bytes 1572872 | tf_op jit(solution)/shard_map/ppermute | solution.py:246
  27.0 13.4 %collective-permute-start.16 = (f32[4,4,64,128]{3,2,1,0:T(8,128)S(1)}, f32[4,4,64,128]{3,2,1,0:T(8,128)S(1)}, u32[]{:S(2)}, u32[]{:S(2)}) collective-permute-start(f32[4,4,64,128]{3,2,1,0:T(8,128)S(1)} %pad_maximum_fusion.1.refs_0_), channel_id=1, source_target_pairs={{0,192},{8,200},{16,208},{24,216},{32,224},{40,232},{48,240},{56,2... | collective-permute-start | bytes 1572872 | tf_op jit(solution)/shard_map/ppermute | solution.py:246
  27.8 14.4 %collective-permute-start.7 = (f32[4,2,128,128]{3,2,1,0:T(8,128)S(1)}, f32[4,2,128,128]{3,2,1,0:T(8,128)S(1)}, u32[]{:S(2)}, u32[]{:S(2)}) collective-permute-start(f32[4,2,128,128]{3,2,1,0:T(8,128)S(1)} %pad_maximum_fusion.refs_0_), channel_id=1, source_target_pairs={{0,8},{8,0},{16,24},{24,16},{32,40},{40,32},{48,56},{56,48},{64,72... | collective-permute-start | bytes 1572872 | tf_op jit(solution)/shard_map/ppermute | solution.py:289
  31.3 14.9 %collective-permute-start.15 = (f32[4,4,64,128]{3,2,1,0:T(8,128)S(1)}, f32[4,4,64,128]{3,2,1,0:T(8,128)S(1)}, u32[]{:S(2)}, u32[]{:S(2)}) collective-permute-start(f32[4,4,64,128]{3,2,1,0:T(8,128)S(1)} %pad_maximum_fusion.1.refs_0_), channel_id=1, source_target_pairs={{0,64},{8,72},{16,80},{24,88},{32,96},{40,104},{48,112},{56,120},{... | collective-permute-start | bytes 1572872 | tf_op jit(solution)/shard_map/ppermute | solution.py:246
  36.7 9.5 %collective-permute-start.6 = (f32[2,2,128,128]{3,2,1,0:T(8,128)S(1)}, f32[2,2,128,128]{3,2,1,0:T(8,128)S(1)}, u32[]{:S(2)}, u32[]{:S(2)}) collective-permute-start(f32[2,2,128,128]{3,2,1,0:T(8,128)S(1)} %slice.25), channel_id=1, source_target_pairs={{0,48},{8,56},{16,0},{24,8},{32,16},{40,24},{48,32},{56,40},{64,11... | collective-permute-start | bytes 786440 | tf_op jit(solution)/shard_map/ppermute | solution.py:246
  40.4 14.5 %collective-permute-start.9 = (f32[4,2,128,128]{3,2,1,0:T(8,128)S(1)}, f32[4,2,128,128]{3,2,1,0:T(8,128)S(1)}, u32[]{:S(2)}, u32[]{:S(2)}) collective-permute-start(f32[4,2,128,128]{3,2,1,0:T(8,128)S(1)} %collective-permute-done.4.refs_2_), channel_id=1, source_target_pairs={{0,8},{8,0},{16,24},{24,16},{32,40},{40,32},{48,56},{56,48},{64,72... | collective-permute-start | bytes 1572872 | tf_op jit(solution)/shard_map/ppermute | solution.py:289
  42.2 12.8 %collective-permute-start.8 = (f32[4,2,128,128]{3,2,1,0:T(8,128)S(1)}, f32[4,2,128,128]{3,2,1,0:T(8,128)S(1)}, u32[]{:S(2)}, u32[]{:S(2)}) collective-permute-start(f32[4,2,128,128]{3,2,1,0:T(8,128)S(1)} %collective-permute-done.3.refs_1_), channel_id=1, source_target_pairs={{0,8},{8,0},{16,24},{24,16},{32,40},{40,32},{48,56},{56,48},{64,72... | collective-permute-start | bytes 1572872 | tf_op jit(solution)/shard_map/ppermute | solution.py:289
  46.2 8.7 %collective-permute-start.17 = (f32[2,4,64,128]{3,2,1,0:T(8,128)S(1)}, f32[2,4,64,128]{3,2,1,0:T(8,128)}, u32[]{:S(2)}, u32[]{:S(2)}) collective-permute-start(f32[2,4,64,128]{3,2,1,0:T(8,128)S(1)} %slice.26), channel_id=1, source_target_pairs={{0,64},{8,72},{16,80},{24,88},{32,96},{40,104},{48,112},{56,120},{... | collective-permute-start | bytes 786440 | tf_op jit(solution)/shard_map/ppermute | solution.py:246
  56.1 8.6 %collective-permute-start.19 = (f32[4,4,64,128]{3,2,1,0:T(8,128)S(1)}, f32[4,4,64,128]{3,2,1,0:T(8,128)}, u32[]{:S(2)}, u32[]{:S(2)}) collective-permute-start(f32[4,4,64,128]{3,2,1,0:T(8,128)S(1)} %pad_maximum_fusion.1.refs_0_), channel_id=1, source_target_pairs={{0,8},{8,0},{16,24},{24,16},{32,40},{40,32},{48,56},{56,48},{64,72... | collective-permute-start | bytes 1572872 | tf_op jit(solution)/shard_map/ppermute | solution.py:291
  56.7 8.0 %collective-permute-start.20 = (f32[4,4,64,128]{3,2,1,0:T(8,128)S(1)}, f32[4,4,64,128]{3,2,1,0:T(8,128)}, u32[]{:S(2)}, u32[]{:S(2)}) collective-permute-start(f32[4,4,64,128]{3,2,1,0:T(8,128)S(1)} %collective-permute-done.15.refs_1_), channel_id=1, source_target_pairs={{0,8},{8,0},{16,24},{24,16},{32,40},{40,32},{48,56},{56,48},{64,72... | collective-permute-start | bytes 1572872 | tf_op jit(solution)/shard_map/ppermute | solution.py:291
  56.8 7.9 %collective-permute-start.21 = (f32[4,4,64,128]{3,2,1,0:T(8,128)S(1)}, f32[4,4,64,128]{3,2,1,0:T(8,128)}, u32[]{:S(2)}, u32[]{:S(2)}) collective-permute-start(f32[4,4,64,128]{3,2,1,0:T(8,128)S(1)} %collective-permute-done.16.refs_2_), channel_id=1, source_target_pairs={{0,8},{8,0},{16,24},{24,16},{32,40},{40,32},{48,56},{56,48},{64,72... | collective-permute-start | bytes 1572872 | tf_op jit(solution)/shard_map/ppermute | solution.py:291
  64.7 16.6 %collective-permute-start.27 = (f32[128,256]{1,0:T(8,128)}, f32[128,256]{1,0:T(8,128)S(1)}, u32[]{:S(2)}, u32[]{:S(2)}) collective-permute-start(f32[128,256]{1,0:T(8,128)} %get-tuple-element.69.refs_0_), channel_id=1, source_target_pairs={{0,6},{1,7},{2,0},{3,1},{4,2},{5,3},{6,4},{7,5},{8,14},{9,15},{10,... | collective-permute-start | bytes 393224 | tf_op jit(solution)/shard_map/ppermute | solution.py:256
  70.7 10.6 %collective-permute-start.26 = (f32[128,256]{1,0:T(8,128)}, f32[128,256]{1,0:T(8,128)S(1)}, u32[]{:S(2)}, u32[]{:S(2)}) collective-permute-start(f32[128,256]{1,0:T(8,128)} %get-tuple-element.69.refs_0_), channel_id=1, source_target_pairs={{0,2},{1,3},{2,4},{3,5},{4,6},{5,7},{6,0},{7,1},{8,10},{9,11},{10,... | collective-permute-start | bytes 393224 | tf_op jit(solution)/shard_map/ppermute | solution.py:256
  70.8 10.7 %collective-permute-start.25 = (f32[128,256]{1,0:T(8,128)}, f32[128,256]{1,0:T(8,128)S(1)}, u32[]{:S(2)}, u32[]{:S(2)}) collective-permute-start(f32[128,256]{1,0:T(8,128)} %get-tuple-element.69.refs_0_), channel_id=1, source_target_pairs={{0,7},{1,0},{2,1},{3,2},{4,3},{5,4},{6,5},{7,6},{8,15},{9,8},{10,9... | collective-permute-start | bytes 393224 | tf_op jit(solution)/shard_map/ppermute | solution.py:256
  74.0 9.4 %collective-permute-start.24 = (f32[128,256]{1,0:T(8,128)}, f32[128,256]{1,0:T(8,128)S(1)}, u32[]{:S(2)}, u32[]{:S(2)}) collective-permute-start(f32[128,256]{1,0:T(8,128)} %get-tuple-element.69.refs_0_), channel_id=1, source_target_pairs={{0,1},{1,2},{2,3},{3,4},{4,5},{5,6},{6,7},{7,0},{8,9},{9,10},{10,1... | collective-permute-start | bytes 393224 | tf_op jit(solution)/shard_map/ppermute | solution.py:256
  83.4 8.8 %collective-permute-start.28 = (f32[128,256]{1,0:T(8,128)S(1)}, f32[128,256]{1,0:T(8,128)S(1)}, u32[]{:S(2)}, u32[]{:S(2)}) collective-permute-start(f32[128,256]{1,0:T(8,128)S(1)} %collective-permute-done.26.refs_3_), channel_id=1, source_target_pairs={{0,1},{1,2},{2,3},{3,4},{4,5},{5,6},{6,7},{7,0},{8,9},{9,10},{10,1... | collective-permute-start | bytes 393224 | tf_op jit(solution)/shard_map/ppermute | solution.py:256
  83.4 8.8 %collective-permute-start.29 = (f32[128,256]{1,0:T(8,128)S(1)}, f32[128,256]{1,0:T(8,128)S(1)}, u32[]{:S(2)}, u32[]{:S(2)}) collective-permute-start(f32[128,256]{1,0:T(8,128)S(1)} %collective-permute-done.27.refs_4_), channel_id=1, source_target_pairs={{0,7},{1,0},{2,1},{3,2},{4,3},{5,4},{6,5},{7,6},{8,15},{9,8},{10,9... | collective-permute-start | bytes 393224 | tf_op jit(solution)/shard_map/ppermute | solution.py:256
  (31 other events, 323.0 us)
Sparse Core Ops, SparseCore 0:
  9.8 42.4 all-gather.2

commit v3 on v2

v3 whole, which is shorter than its diff:
```python
import jax
import jax.numpy as jnp
from jax import lax
from jax.experimental import pallas as pl
from jax.experimental.pallas import tpu as pltpu
from jax.sharding import PartitionSpec as P

BLOCK_ROWS = 32
PAIRS = [(i, i ^ 1) for i in range(32)]
SAME_CORE = [[2 * m + k for m in range(16)] for k in range(2)]
f32 = jnp.float32
bf16 = jnp.bfloat16

VMEM = pl.BlockSpec(memory_space=pltpu.VMEM)
ANY = pl.BlockSpec(memory_space=pl.ANY)
HBM = pl.BlockSpec(memory_space=pltpu.HBM)
SMEM = pl.BlockSpec(memory_space=pltpu.SMEM)


def call(kernel, outs, ins, cost, scratch=(), mib=60):
    return pl.pallas_call(
        kernel,
        out_shape=[jax.ShapeDtypeStruct(*out) for out in outs],
        in_specs=ins,
        out_specs=[VMEM] * len(outs),
        scratch_shapes=list(scratch),
        compiler_params=pltpu.CompilerParams(vmem_limit_bytes=60 * 1024 * 1024),
        cost_estimate=pl.CostEstimate(flops=cost[0], bytes_accessed=cost[1], transcendentals=0),
    )


def split(x):
    high = x.astype(bf16)
    return high, (x - high.astype(f32)).astype(bf16)


def dot(a, b):
    return jnp.dot(a, b, preferred_element_type=f32)


def product(x, high, low):
    up, down = split(x)
    rows = x.shape[0]
    both = dot(jnp.concatenate([up, down], axis=0), high)
    return both[:rows] + both[rows:] + dot(up, low)


def squares(x):
    return jnp.sum(x * x, axis=0, keepdims=True)


def kids_in_order(parents):
    order = []
    for which in range(2):
        hit = [parents[j] == which for j in range(4)]
        order.append(jnp.where(hit[0], 0, jnp.where(hit[1], 1, 2)))
        order.append(jnp.where(hit[3], 3, jnp.where(hit[2], 2, 1)))
    return order


def pack_kernel(root_inv, level1, panel, child, out, panels, children):
    out[0:128, :] = root_inv[...]
    for which in range(2):
        apart = panel[pl.ds(which, 128, stride=2), :]
        for n in range(16):
            panels[n, which] = apart
    whole = child[...]
    for n in range(16):
        children[n] = whole
    for q in range(4):
        out[128:144, 128 * q : 128 * q + 128] = level1[16 * q : 16 * q + 16, :]


def chip_of(ids):
    return ids[2] // 8, (ids[2] // 2) % 4


def fetch_rows(ids, parts, factor, tail, arrived):
    copies = []
    for n, away in enumerate((0, 1, 2, 3, 4, 7, 6, 5)):
        z = (ids[1] + 8 - away) % 8
        copies.append(
            pltpu.make_async_copy(parts[n].at[pl.ds(0, 128)], factor.at[z], arrived.at[n])
        )
        if tail is not None:
            copies.append(
                pltpu.make_async_copy(
                    parts[n].at[pl.ds(128, 16)], tail.at[z], arrived.at[8 + n]
                )
            )
    return copies


def split_rows(copies, factor, both):
    for copy in copies:
        copy.wait()
    for z in range(8):
        high, low = split(factor[z])
        both[0:128, 512 * z : 512 * z + 512] = high
        both[128:256, 512 * z : 512 * z + 512] = low


def times_rows(both, high, low):
    first = dot(both[...], high)
    return first[:128] + first[128:] + dot(both[0:128, :], low)


def cross_kernel(ids, *refs):
    parts, sides, refs = refs[:8], refs[8:10], refs[10:]
    cross, root, factor, panels, both, high, low, row_here, panel_here = refs
    row_copies = fetch_rows(ids, parts, factor, None, row_here)
    copies = [
        pltpu.make_async_copy(side, panels.at[n], panel_here.at[n])
        for n, side in enumerate(sides)
    ]
    for copy in copies + row_copies:
        copy.start()
    for n, copy in enumerate(copies):
        copy.wait()
        core = ids[0] if n == 0 else 1 - ids[0]
        for chip in range(16):
            spot = pl.ds(pl.multiple_of(128 * (2 * chip + core), 128), 128)
            for which in range(2):
                up, down = split(panels[n, chip, which])
                high[spot, 128 * which : 128 * which + 128] = up
                low[spot, 128 * which : 128 * which + 128] = down
    split_rows(row_copies, factor, both)
    for z in range(8):
        root[z] = squares(factor[z])
    cross[...] = times_rows(both, high[...], low[...])


def child_kernel(ids, parents, widths, blocks, child_inv, *refs):
    rows, sides, refs = refs[:8], refs[8:10], refs[10:]
    image, below_high, below_low, base, lines = refs[:5]
    factor, level1, panels, both, high, low, row_here, part_here = refs[5:]
    copies = [
        pltpu.make_async_copy(side, panels.at[n], part_here.at[n])
        for n, side in enumerate(sides)
    ]
    row_copies = fetch_rows(ids, rows, factor, level1, row_here)
    for copy in copies + row_copies:
        copy.start()
    high[...] = jnp.zeros_like(high)
    low[...] = jnp.zeros_like(low)
    lanes = ids[1] * 128 + lax.broadcasted_iota(jnp.int32, (32, 128), 1)
    order = kids_in_order(parents)
    live = [lanes < widths[kid] for kid in order]
    for n, copy in enumerate(copies):
        copy.wait()
        core = ids[0] if n == 0 else 1 - ids[0]
        for chip in range(16):
            for half in range(2):
                slot = 4 * chip + 2 * core + half
                for place, kid in enumerate(order):
                    row = pl.multiple_of(blocks[kid, slot] * BLOCK_ROWS, BLOCK_ROWS)
                    piece = panels[n, chip, kid, 32 * half : 32 * half + 32, :]
                    up, down = split(jnp.where(live[place], piece, 0.0))
                    high[pl.ds(row, 32), 128 * place : 128 * place + 128] = up
                    low[pl.ds(row, 32), 128 * place : 128 * place + 128] = down
    split_rows(row_copies, factor, both)
    image[...] = times_rows(both, high[0:4096, :], low[0:4096, :])
    below_high[...] = high[4096:5120, :]
    below_low[...] = low[4096:5120, :]

    depth = ids[2] * 32 + lax.broadcasted_iota(jnp.int32, (32, 128), 0)
    for j in range(4):
        inside = jnp.logical_and(depth < widths[j], lanes < widths[j])
        base[j : j + 1, :] = squares(jnp.where(inside, child_inv[j], 0.0))
    own = jnp.concatenate(
        [
            jnp.concatenate([level1[n, :, 128 * q : 128 * q + 128] for n in range(8)], axis=1)
            for q in range(4)
        ],
        axis=0,
    )
    lower = product(own, high[4096:5120, :], low[4096:5120, :])
    parity = lax.broadcasted_iota(jnp.int32, (64, 1024), 0) % 2
    parity_half = lax.broadcasted_iota(jnp.int32, (64, 256), 0) % 2
    for which in range(2):
        half = slice(256 * which, 256 * which + 256)
        sums = squares(jnp.where(parity_half == which, lower[:, half], 0.0))
        base[...] += by_child(parents, which, sums)
        lines[which : which + 1, :] = squares(jnp.where(parity == which, own, 0.0))


def by_child(parents, which, sums):
    place = lax.broadcasted_iota(jnp.int32, (4, 128), 0)
    first, second = kids_in_order(parents)[2 * which : 2 * which + 2]
    return jnp.where(place == first, sums[:, :128], 0.0) + jnp.where(
        place == second, sums[:, 128:], 0.0
    )


def finish_kernel(ids, parents, root, base, lines, image, below_high, below_low, *refs):
    parts, (payload, cross, arrived) = refs[:8], refs[8:]
    copies = []
    for n, away in enumerate((0, 1, 7, 2, 6, 4, 3, 5)):
        spot = cross.at[(ids[1] + 8 - away) % 8]
        copies.append(pltpu.make_async_copy(parts[n], spot, arrived.at[n]))
    for copy in copies:
        copy.start()
    for copy in copies:
        copy.wait()
    ends = base[...]
    known_lines = []
    for which in range(2):
        half = slice(256 * which, 256 * which + 256)
        known = jnp.concatenate(
            [cross[z, :, 128 * which : 128 * which + 128] for z in range(8)], axis=1
        )
        upper = image[:, half] - product(known, below_high[:, half], below_low[:, half])
        ends = ends + by_child(parents, which, squares(upper))
        known_lines.append(lines[which : which + 1, :] + squares(known))
    for i in range(32):
        b = i // 4
        payload[i, 0:4, :] = ends
        payload[i, 4:5, :] = root[b, :, 128 * (i % 4) : 128 * (i % 4) + 128]
        payload[i, 5:6, :] = known_lines[0][:, 128 * b : 128 * b + 128]
        payload[i, 6:7, :] = known_lines[1][:, 128 * b : 128 * b + 128]
        payload[i, 7:8, :] = jnp.zeros((1, 128), f32)


def sum_kernel(ids, parts, root, parent, child):
    total = parts[0]
    for i in range(1, 32):
        total = total + parts[i]
    child[...] = total[0:4, :]
    root[...] = total[4:5, :]
    place = ids[2] % 4
    found = total[5:7, 0:32]
    for n in range(1, 4):
        found = jnp.where(place == n, total[5:7, 32 * n : 32 * n + 32], found)
    parent[...] = found


def moved(x, down, right):
    def target(i):
        y, x, core = i // 8, i // 2 % 4, i % 2
        return ((y + down) % 4 * 4 + (x + right) % 4) * 2 + core

    return lax.ppermute(x, "row", [(i, target(i)) for i in range(32)])


def along(x, n):
    return lax.ppermute(x, "col", [(z, (z + n) % 8) for z in range(8)])


def body(
    root_inv,
    level1_inv,
    level1_panel,
    child_inv,
    child_panel,
    child_width,
    child_parent,
    child_blocks,
):
    row = lax.axis_index("row")
    col = lax.axis_index("col")
    ids = jnp.stack([row & 1, col, row]).astype(jnp.int32)

    packed, panels, children = call(
        pack_kernel,
        [((144, 512), f32), ((16, 2, 128, 128), f32), ((16, 4, 64, 128), f32)],
        [VMEM] * 4, (0, 5_000_000),
    )(root_inv, level1_inv.reshape(64, 128), level1_panel.reshape(256, 128), child_panel)
    fence = lax.optimization_barrier
    down, up = [packed], [packed]
    for n in range(3):
        down.append(along(down[-1], 1))
        up.append(along(up[-1], -1))
    mine = lax.all_to_all(
        panels, "row", 0, 0, tiled=True, axis_index_groups=SAME_CORE
    )
    mine, children, down[3], up[3] = fence((mine, children, down[3], up[3]))
    rows = down + [along(down[3], 1)] + up[1:]
    panels = [mine, lax.ppermute(mine, "row", PAIRS)]
    mine = lax.all_to_all(
        children, "row", 0, 0, tiled=True, axis_index_groups=SAME_CORE
    )

    cross, root = call(
        cross_kernel, [((128, 256), f32), ((8, 1, 512), f32)],
        [SMEM] + [HBM] * 8 + [ANY, HBM], (40_000_000_000, 6_000_000),
        [
            pltpu.VMEM((8, 128, 512), f32),
            pltpu.VMEM((2, 16, 2, 128, 128), f32),
            pltpu.VMEM((256, 4096), bf16),
            pltpu.VMEM((4096, 256), bf16),
            pltpu.VMEM((4096, 256), bf16),
            pltpu.SemaphoreType.DMA((8,)),
            pltpu.SemaphoreType.DMA((2,)),
        ],
        32,
    )(ids, *rows, *panels)
    crosses = [along(cross, n) for n in (1, -1, 2, -2, 4)]
    crosses = [cross] + crosses + [along(crosses[2], 1), along(crosses[3], -1)]
    mine, _ = fence((mine, crosses))
    children = [mine, lax.ppermute(mine, "row", PAIRS)]

    image, below_high, below_low, base, lines = call(
        child_kernel,
        [
            ((128, 512), f32), ((1024, 512), bf16), ((1024, 512), bf16),
            ((4, 128), f32), ((2, 1024), f32),
        ],
        [SMEM] * 4 + [VMEM] + [HBM] * 8 + [ANY, HBM], (1_600_000_000, 10_000_000),
        [
            pltpu.VMEM((8, 128, 512), f32),
            pltpu.VMEM((8, 16, 512), f32),
            pltpu.VMEM((2, 16, 4, 64, 128), f32),
            pltpu.VMEM((256, 4096), bf16),
            pltpu.VMEM((5120, 512), bf16),
            pltpu.VMEM((5120, 512), bf16),
            pltpu.SemaphoreType.DMA((16,)),
            pltpu.SemaphoreType.DMA((2,)),
        ],
        30,
    )(ids, child_parent, child_width, child_blocks, child_inv, *rows, *children)

    (payload,) = call(
        finish_kernel, [((32, 8, 128), f32)], [SMEM] * 2 + [VMEM] * 6 + [ANY] * 8,
        (500_000_000, 3_000_000),
        [pltpu.VMEM((8, 128, 256), f32), pltpu.SemaphoreType.DMA((8,))],
        16,
    )(ids, child_parent, root, base, lines, image, below_high, below_low, *crosses)
    root, parent, child = call(
        sum_kernel, [((1, 128), f32), ((2, 32), f32), ((4, 128), f32)], [SMEM, VMEM],
        (0, 130_000), (), 16,
    )(ids, lax.all_to_all(payload, "row", 0, 0, tiled=True))
    return root.reshape(128), parent, child


def solution(mesh):
    placed = (
        P("row", "col"),
        P("row", None, "col"),
        P("row", None, "col"),
        P(None, "row", "col"),
        P(None, "row", "col"),
        P(),
        P(),
        P(),
    )
    return jax.shard_map(
        body,
        mesh=mesh,
        in_specs=placed,
        out_specs=(P("row"), P(None, "row"), P(None, "col")),
        check_vma=False,
    )
```

time: 121 us -> 117 us (0.967)
  waiting for transfers between devices: 21.2 us -> 38.8 us
  between operations: 14.4 us -> 0.81 us
  starting transfers between devices: 45.6 us -> 41.3 us
  blocking collectives: 15.1 us -> 12.3 us
  other arithmetic: 2.54 us -> 0.67 us
    ppermute x32 -> x16, starting transfers between devices: 45.6 us -> 28.1 us  [the longest x14 24.2 us: along(): return lax.ppermute(x, 'col', [(z, (z + n) % 8) for z in range(8)])]
    all_to_all x0 -> x2, starting transfers between devices: none -> 13.2 us  [the longest x1 7.77 us: body(): lax.all_to_all(panels, 'row', 0, 0, tiled=True, axis_index_groups=SAME_CORE)]
    all_to_all x0 -> x2, waiting for transfers between devices: none -> 12.5 us  [the longest x1 11.4 us: body(): lax.all_to_all(children, 'row', 0, 0, tiled=True, axis_index_groups=SAME_...]
    ppermute x32 -> x16, waiting for transfers between devices: 21.2 us -> 26.3 us  [the longest x14 22.4 us: along(): return lax.ppermute(x, 'col', [(z, (z + n) % 8) for z in range(8)])]
    all_to_all x1, blocking collectives: 15.1 us -> 12.3 us  [body(): lax.all_to_all(payload, 'row', 0, 0, tiled=True)]
    another operation x2 -> x0, other arithmetic: 1.88 us -> none  [the longest x1 0.95 us: body(): jnp.stack([child_panel] + [moved(child_panel, 0, n) for n in (1, 2, 3)])]
    pallas_call x1, Pallas kernels: 1.79 us -> 3.36 us  [body(): call(pack_kernel, [((144, 512), f32), ((16, 2, 128, 128), f32), ((16, 4,...]
  transfers between devices with their start and end apart: 33 -> 18, of which waited for: 10 -> 11; matrix products, arithmetic and copies ran while one was open for 2% -> 1% of each run, Pallas kernels for 11% -> 4%
where the time goes in v3:
time: 117 us
  starting transfers between devices  41.3 us (35%)
  waiting for transfers between devices  38.8 us (33%)
  Pallas kernels  21.9 us (19%)
  blocking collectives  12.3 us (11%)
    ppermute x14, starting transfers between devices, along(): return lax.ppermute(x, 'col', [(z, (z + n) % 8) for z in range(8)])  24.2 us
    ppermute x14, waiting for transfers between devices, along(): return lax.ppermute(x, 'col', [(z, (z + n) % 8) for z in range(8)])  22.4 us
    all_to_all x1, blocking collectives, body(): lax.all_to_all(payload, 'row', 0, 0, tiled=True)  12.3 us
    all_to_all x1, waiting for transfers between devices, body(): lax.all_to_all(children, 'row', 0, 0, tiled=True, axis_index_groups=SAME_...  11.4 us
    all_to_all x1, starting transfers between devices, body(): lax.all_to_all(panels, 'row', 0, 0, tiled=True, axis_index_groups=SAME_CORE)  7.77 us
    pallas_call x1, Pallas kernels, body(): call(child_kernel, [((128, 512), f32), ((1024, 512), bf16), ((1024, 512),...  7.24 us
    all_to_all x1, starting transfers between devices, body(): lax.all_to_all(children, 'row', 0, 0, tiled=True, axis_index_groups=SAME_...  5.42 us
    pallas_call x1, Pallas kernels, body(): call(cross_kernel, [((128, 256), f32), ((8, 1, 512), f32)], [SMEM] + [HBM...  5.18 us
  transfers between devices with their start and end apart: 18, of which 11 were waited for; matrix products, arithmetic and copies ran while one was open for 1% of the time, Pallas kernels for 4%

profile of v3, /device:TPU:1, one launch (start us, length us, event | category | flops | bytes accessed | tf_op | source)
XLA Modules:
  0.0 116.5 jit_solution(11414086807223821540)
XLA Ops:
  0.6 3.4 %shard_map.103 = (f32[144,512]{1,0:T(8,128)}, f32[16,2,128,128]{3,2,1,0:T(8,128)}, f32[16,4,64,128]{3,2,1,0:T(8,128)}) custom-call(f32[128,512]{1,0:T(8,128)} %root_inv.1, f32[64,128]{1,0:T(8,128)} %bitcast.7, f32[256,128]{1,0:T(8,128)} %bitcast.6, f32[4,64,128]{2,1,0:T(8,128)} %child.1), custom_call_target="tpu_custom_call" | custom-call | bytes 5000000 | tf_op jit(solution)/shard_map/pallas_call | solution.py:263
  4.0 7.8 %all-to-all-start = ((f32[16,2,128,128]{3,2,1,0:T(8,128)}), f32[16,2,128,128]{3,2,1,0:T(8,128)}, u32[]{:S(2)}, u32[]{:S(2)}) async-start(f32[16,2,128,128]{3,2,1,0:T(8,128)} %get-tuple-element.22), calls=%async_computation | async-start | bytes 4194304 | tf_op jit(solution)/shard_map/all_to_all | solution.py:273
  11.8 5.7 %collective-permute-start.3 = (f32[144,512]{1,0:T(8,128)S(1)}, f32[144,512]{1,0:T(8,128)S(1)}, u32[]{:S(2)}, u32[]{:S(2)}) collective-permute-start(f32[144,512]{1,0:T(8,128)S(1)} %copy-done.1), channel_id=1, source_target_pairs={{0,7},{1,0},{2,1},{3,2},{4,3},{5,4},{6,5},{7,6},{8,15},{9,8},{10,9... | collective-permute-start | bytes 884744 | tf_op jit(solution)/shard_map/ppermute | solution.py:246
  17.4 5.4 %collective-permute-done.3.refs_5_ = f32[144,512]{1,0:T(8,128)S(1)} collective-permute-done((f32[144,512]{1,0:T(8,128)S(1)}, f32[144,512]{1,0:T(8,128)S(1)}, u32[]{:S(2)}, u32[]{:S(2)}) %collective-permute-start.3) | collective-permute-done | bytes 294944 | tf_op jit(solution)/shard_map/ppermute | solution.py:246
  22.8 3.5 %collective-permute-start.4 = (f32[144,512]{1,0:T(8,128)S(1)}, f32[144,512]{1,0:T(8,128)S(1)}, u32[]{:S(2)}, u32[]{:S(2)}) collective-permute-start(f32[144,512]{1,0:T(8,128)S(1)} %collective-permute-done.3.refs_5_), channel_id=1, source_target_pairs={{0,7},{1,0},{2,1},{3,2},{4,3},{5,4},{6,5},{7,6},{8,15},{9,8},{10,9... | collective-permute-start | bytes 884744 | tf_op jit(solution)/shard_map/ppermute | solution.py:246
  26.3 4.5 %collective-permute-done.4.refs_6_ = f32[144,512]{1,0:T(8,128)S(1)} collective-permute-done((f32[144,512]{1,0:T(8,128)S(1)}, f32[144,512]{1,0:T(8,128)S(1)}, u32[]{:S(2)}, u32[]{:S(2)}) %collective-permute-start.4) | collective-permute-done | bytes 294944 | tf_op jit(solution)/shard_map/ppermute | solution.py:246
  30.9 3.5 %collective-permute-start.5 = (f32[144,512]{1,0:T(8,128)S(1)}, f32[144,512]{1,0:T(8,128)S(1)}, u32[]{:S(2)}, u32[]{:S(2)}) collective-permute-start(f32[144,512]{1,0:T(8,128)S(1)} %collective-permute-done.4.refs_6_), channel_id=1, source_target_pairs={{0,7},{1,0},{2,1},{3,2},{4,3},{5,4},{6,5},{7,6},{8,15},{9,8},{10,9... | collective-permute-start | bytes 884744 | tf_op jit(solution)/shard_map/ppermute | solution.py:246
  34.4 3.7 %collective-permute-done.5.refs_7_ = f32[144,512]{1,0:T(8,128)S(1)} collective-permute-done((f32[144,512]{1,0:T(8,128)S(1)}, f32[144,512]{1,0:T(8,128)S(1)}, u32[]{:S(2)}, u32[]{:S(2)}) %collective-permute-start.5) | collective-permute-done | bytes 294944 | tf_op jit(solution)/shard_map/ppermute | solution.py:246
  38.8 2.5 %collective-permute-done.2.refs_3_ = f32[144,512]{1,0:T(8,128)} collective-permute-done((f32[144,512]{1,0:T(8,128)S(1)}, f32[144,512]{1,0:T(8,128)}, u32[]{:S(2)}, u32[]{:S(2)}) %collective-permute-start.2) | collective-permute-done | bytes 294944 | tf_op jit(solution)/shard_map/ppermute | solution.py:246
  41.3 1.0 all-to-all-done.refs_8_
  42.3 3.0 %collective-permute-start.7 = (f32[16,2,128,128]{3,2,1,0:T(8,128)}, f32[16,2,128,128]{3,2,1,0:T(8,128)}, u32[]{:S(2)}, u32[]{:S(2)}) collective-permute-start(f32[16,2,128,128]{3,2,1,0:T(8,128)} %all-to-all-done.refs_8_), channel_id=1, source_target_pairs={{0,8},{8,0},{16,24},{24,16},{32,40},{40,32},{48,56},{56,48},{64,72... | collective-permute-start | bytes 6291464 | tf_op jit(solution)/shard_map/ppermute | solution.py:278
  46.8 5.4 %all-to-all-start.1 = ((f32[16,4,64,128]{3,2,1,0:T(8,128)}), f32[16,4,64,128]{3,2,1,0:T(8,128)S(1)}, u32[]{:S(2)}, u32[]{:S(2)}) async-start(f32[16,4,64,128]{3,2,1,0:T(8,128)} %get-tuple-element.28), calls=%async_computation.1 | async-start | bytes 4194304 | tf_op jit(solution)/shard_map/all_to_all | solution.py:279
  52.2 5.5 %collective-permute-done.6.refs_4_ = f32[144,512]{1,0:T(8,128)} collective-permute-done((f32[144,512]{1,0:T(8,128)}, f32[144,512]{1,0:T(8,128)}, u32[]{:S(2)}, u32[]{:S(2)}) %collective-permute-start.6) | collective-permute-done | bytes 294944 | tf_op jit(solution)/shard_map/ppermute | solution.py:246
  57.7 5.2 %shard_map.104 = (f32[128,256]{1,0:T(8,128)}, f32[8,1,512]{2,1,0:T(1,128)}) custom-call(s32[3]{0:T(128)} %pad_add_fusion.ids, f32[144,512]{1,0:T(8,128)} %get-tuple-element.21.refs_0_, f32[144,512]{1,0:T(8,128)} %copy-done.3, f32[144,512]{1,0:T(8,128)} %copy-done.5, f32[144,512]{1,0:T(8,128)} %collective-permute-done.2.refs_3_, ...), custom_call_target="tpu_custom_call" | custom-call | flops 40000000000 | bytes 6000000 | tf_op jit(solution)/shard_map/pallas_call | solution.py:283
  62.9 1.8 %collective-permute-start.11 = (f32[128,256]{1,0:T(8,128)}, f32[128,256]{1,0:T(8,128)S(1)}, u32[]{:S(2)}, u32[]{:S(2)}) collective-permute-start(f32[128,256]{1,0:T(8,128)} %get-tuple-element.29.refs_0_), channel_id=1, source_target_pairs={{0,6},{1,7},{2,0},{3,1},{4,2},{5,3},{6,4},{7,5},{8,14},{9,15},{10,... | collective-permute-start | bytes 393224 | tf_op jit(solution)/shard_map/ppermute | solution.py:246
  65.3 3.8 %collective-permute-start.12 = (f32[128,256]{1,0:T(8,128)}, f32[128,256]{1,0:T(8,128)S(1)}, u32[]{:S(2)}, u32[]{:S(2)}) collective-permute-start(f32[128,256]{1,0:T(8,128)} %get-tuple-element.29.refs_0_), channel_id=1, source_target_pairs={{0,4},{1,5},{2,6},{3,7},{4,0},{5,1},{6,2},{7,3},{8,12},{9,13},{10,... | collective-permute-start | bytes 393224 | tf_op jit(solution)/shard_map/ppermute | solution.py:246
  69.6 1.0 collective-permute-start.8
  70.7 3.0 %collective-permute-start.14 = (f32[128,256]{1,0:T(8,128)S(1)}, f32[128,256]{1,0:T(8,128)S(1)}, u32[]{:S(2)}, u32[]{:S(2)}) collective-permute-start(f32[128,256]{1,0:T(8,128)S(1)} %collective-permute-done.11.refs_4_), channel_id=1, source_target_pairs={{0,7},{1,0},{2,1},{3,2},{4,3},{5,4},{6,5},{7,6},{8,15},{9,8},{10,9... | collective-permute-start | bytes 393224 | tf_op jit(solution)/shard_map/ppermute | solution.py:246
  74.1 11.4 %all-to-all-done.1.refs_8_ = f32[16,4,64,128]{3,2,1,0:T(8,128)S(1)} async-done(((f32[16,4,64,128]{3,2,1,0:T(8,128)}), f32[16,4,64,128]{3,2,1,0:T(8,128)S(1)}, u32[]{:S(2)}, u32[]{:S(2)}) %all-to-all-start.1) | async-done | bytes 2097184 | tf_op jit(solution)/shard_map/all_to_all | solution.py:279
  86.8 3.9 %collective-permute-done.15.refs_9_ = f32[16,4,64,128]{3,2,1,0:T(8,128)} collective-permute-done((f32[16,4,64,128]{3,2,1,0:T(8,128)S(1)}, f32[16,4,64,128]{3,2,1,0:T(8,128)}, u32[]{:S(2)}, u32[]{:S(2)}) %collective-permute-start.15) | collective-permute-done | bytes 2097184 | tf_op jit(solution)/shard_map/ppermute | solution.py:300
  90.8 7.2 %shard_map.105 = (f32[128,512]{1,0:T(8,128)}, bf16[1024,512]{1,0:T(8,128)(2,1)}, bf16[1024,512]{1,0:T(8,128)(2,1)}, f32[4,128]{1,0:T(4,128)}, f32[2,1024]{1,0:T(2,128)}) custom-call(s32[3]{0:T(128)} %pad_add_fusion.ids, s32[4]{0:T(128)} %parents.3, s32[4]{0:T(128)} %widths.1, s32[4,64]{1,0:T(4,128)} %blocks.1, f32[4,32,128]{2,1,0:T(8,128)} %child_inv.1, ...), custom_call_target="tpu_custom_call" | custom-call | flops 1600000000 | bytes 10000000 | tf_op jit(solution)/shard_map/pallas_call | solution.py:302
  98.1 4.3 %shard_map.106 = f32[32,8,128]{2,1,0:T(8,128)} custom-call(s32[3]{0:T(128)} %pad_add_fusion.ids, s32[4]{0:T(128)} %parents.3, f32[8,1,512]{2,1,0:T(1,128)} %get-tuple-element.27.root, f32[4,128]{1,0:T(4,128)} %get-tuple-element.31.base, f32[2,1024]{1,0:T(2,128)} %get-tuple-element.32.lines, f32[128,512]{1,0:T(8,128)} %get-tuple-element.33.image, ...), custom_call_target="tpu_custom_call" | custom-call | flops 500000000 | bytes 3000000 | tf_op jit(solution)/shard_map/pallas_call | solution.py:322
  102.4 12.3 %all_to_all.15.parts = f32[32,8,128]{2,1,0:T(8,128)} all-to-all(f32[32,8,128]{2,1,0:T(8,128)} %shard_map.106), channel_id=1, replica_groups=mesh['row'=32,'col'=8] {'row'}, dimensions={0} | all-to-all | bytes 262144 | tf_op jit(solution)/shard_map/all_to_all | solution.py:331
  114.7 1.8 %shard_map.107 = (f32[1,128]{1,0:T(1,128)}, f32[2,32]{1,0:T(2,128)}, f32[4,128]{1,0:T(4,128)}) custom-call(s32[3]{0:T(128)} %pad_add_fusion.ids, f32[32,8,128]{2,1,0:T(8,128)} %all_to_all.15.parts), custom_call_target="tpu_custom_call" | custom-call | bytes 130000 | tf_op jit(solution)/shard_map/pallas_call | solution.py:328
  (47 shorter events, 5.1 us)
Async XLA Ops:
  4.0 38.3 %all-to-all-start = ((f32[16,2,128,128]{3,2,1,0:T(8,128)}), f32[16,2,128,128]{3,2,1,0:T(8,128)}, u32[]{:S(2)}, u32[]{:S(2)}) async-start(f32[16,2,128,128]{3,2,1,0:T(8,128)} %get-tuple-element.22), calls=%async_computation | async-start | bytes 4194304 | tf_op jit(solution)/shard_map/all_to_all | solution.py:273
  11.8 11.0 %collective-permute-start.3 = (f32[144,512]{1,0:T(8,128)S(1)}, f32[144,512]{1,0:T(8,128)S(1)}, u32[]{:S(2)}, u32[]{:S(2)}) collective-permute-start(f32[144,512]{1,0:T(8,128)S(1)} %copy-done.1), channel_id=1, source_target_pairs={{0,7},{1,0},{2,1},{3,2},{4,3},{5,4},{6,5},{7,6},{8,15},{9,8},{10,9... | collective-permute-start | bytes 884744 | tf_op jit(solution)/shard_map/ppermute | solution.py:246
  17.4 8.9 %collective-permute-start = (f32[144,512]{1,0:T(8,128)S(1)}, f32[144,512]{1,0:T(8,128)S(1)}, u32[]{:S(2)}, u32[]{:S(2)}) collective-permute-start(f32[144,512]{1,0:T(8,128)S(1)} %copy-done.1), channel_id=1, source_target_pairs={{0,1},{1,2},{2,3},{3,4},{4,5},{5,6},{6,7},{7,0},{8,9},{9,10},{10,1... | collective-permute-start | bytes 884744 | tf_op jit(solution)/shard_map/ppermute | solution.py:246
  22.8 23.9 %copy-start.2 = (f32[144,512]{1,0:T(8,128)}, f32[144,512]{1,0:T(8,128)S(1)}, u32[]{:S(2)}) copy-start(f32[144,512]{1,0:T(8,128)S(1)} %collective-permute-done.3.refs_5_) | copy-start | bytes 884740
  22.8 8.1 %collective-permute-start.4 = (f32[144,512]{1,0:T(8,128)S(1)}, f32[144,512]{1,0:T(8,128)S(1)}, u32[]{:S(2)}, u32[]{:S(2)}) collective-permute-start(f32[144,512]{1,0:T(8,128)S(1)} %collective-permute-done.3.refs_5_), channel_id=1, source_target_pairs={{0,7},{1,0},{2,1},{3,2},{4,3},{5,4},{6,5},{7,6},{8,15},{9,8},{10,9... | collective-permute-start | bytes 884744 | tf_op jit(solution)/shard_map/ppermute | solution.py:246
  26.3 20.4 %copy-start.3 = (f32[144,512]{1,0:T(8,128)}, f32[144,512]{1,0:T(8,128)S(1)}, u32[]{:S(2)}) copy-start(f32[144,512]{1,0:T(8,128)S(1)} %collective-permute-done.refs_1_) | copy-start | bytes 884740
  26.3 8.1 %collective-permute-start.1 = (f32[144,512]{1,0:T(8,128)S(1)}, f32[144,512]{1,0:T(8,128)S(1)}, u32[]{:S(2)}, u32[]{:S(2)}) collective-permute-start(f32[144,512]{1,0:T(8,128)S(1)} %collective-permute-done.refs_1_), channel_id=1, source_target_pairs={{0,1},{1,2},{2,3},{3,4},{4,5},{5,6},{6,7},{7,0},{8,9},{9,10},{10,1... | collective-permute-start | bytes 884744 | tf_op jit(solution)/shard_map/ppermute | solution.py:246
  30.9 15.9 %copy-start.4 = (f32[144,512]{1,0:T(8,128)}, f32[144,512]{1,0:T(8,128)S(1)}, u32[]{:S(2)}) copy-start(f32[144,512]{1,0:T(8,128)S(1)} %collective-permute-done.4.refs_6_) | copy-start | bytes 884740
  30.9 7.2 %collective-permute-start.5 = (f32[144,512]{1,0:T(8,128)S(1)}, f32[144,512]{1,0:T(8,128)S(1)}, u32[]{:S(2)}, u32[]{:S(2)}) collective-permute-start(f32[144,512]{1,0:T(8,128)S(1)} %collective-permute-done.4.refs_6_), channel_id=1, source_target_pairs={{0,7},{1,0},{2,1},{3,2},{4,3},{5,4},{6,5},{7,6},{8,15},{9,8},{10,9... | collective-permute-start | bytes 884744 | tf_op jit(solution)/shard_map/ppermute | solution.py:246
  34.4 6.9 %collective-permute-start.2 = (f32[144,512]{1,0:T(8,128)S(1)}, f32[144,512]{1,0:T(8,128)}, u32[]{:S(2)}, u32[]{:S(2)}) collective-permute-start(f32[144,512]{1,0:T(8,128)S(1)} %collective-permute-done.1.refs_2_), channel_id=1, source_target_pairs={{0,1},{1,2},{2,3},{3,4},{4,5},{5,6},{6,7},{7,0},{8,9},{9,10},{10,1... | collective-permute-start | bytes 884744 | tf_op jit(solution)/shard_map/ppermute | solution.py:246
  42.3 15.4 %collective-permute-start.7 = (f32[16,2,128,128]{3,2,1,0:T(8,128)}, f32[16,2,128,128]{3,2,1,0:T(8,128)}, u32[]{:S(2)}, u32[]{:S(2)}) collective-permute-start(f32[16,2,128,128]{3,2,1,0:T(8,128)} %all-to-all-done.refs_8_), channel_id=1, source_target_pairs={{0,8},{8,0},{16,24},{24,16},{32,40},{40,32},{48,56},{56,48},{64,72... | collective-permute-start | bytes 6291464 | tf_op jit(solution)/shard_map/ppermute | solution.py:278
  45.3 12.4 %collective-permute-start.6 = (f32[144,512]{1,0:T(8,128)}, f32[144,512]{1,0:T(8,128)}, u32[]{:S(2)}, u32[]{:S(2)}) collective-permute-start(f32[144,512]{1,0:T(8,128)} %collective-permute-done.2.refs_3_), channel_id=1, source_target_pairs={{0,1},{1,2},{2,3},{3,4},{4,5},{5,6},{6,7},{7,0},{8,9},{9,10},{10,1... | collective-permute-start | bytes 884744 | tf_op jit(solution)/shard_map/ppermute | solution.py:246
  46.8 38.8 %all-to-all-start.1 = ((f32[16,4,64,128]{3,2,1,0:T(8,128)}), f32[16,4,64,128]{3,2,1,0:T(8,128)S(1)}, u32[]{:S(2)}, u32[]{:S(2)}) async-start(f32[16,4,64,128]{3,2,1,0:T(8,128)} %get-tuple-element.28), calls=%async_computation.1 | async-start | bytes 4194304 | tf_op jit(solution)/shard_map/all_to_all | solution.py:279
  62.9 7.8 %collective-permute-start.11 = (f32[128,256]{1,0:T(8,128)}, f32[128,256]{1,0:T(8,128)S(1)}, u32[]{:S(2)}, u32[]{:S(2)}) collective-permute-start(f32[128,256]{1,0:T(8,128)} %get-tuple-element.29.refs_0_), channel_id=1, source_target_pairs={{0,6},{1,7},{2,0},{3,1},{4,2},{5,3},{6,4},{7,5},{8,14},{9,15},{10,... | collective-permute-start | bytes 393224 | tf_op jit(solution)/shard_map/ppermute | solution.py:246
  64.7 9.4 %collective-permute-start.10 = (f32[128,256]{1,0:T(8,128)}, f32[128,256]{1,0:T(8,128)S(1)}, u32[]{:S(2)}, u32[]{:S(2)}) collective-permute-start(f32[128,256]{1,0:T(8,128)} %get-tuple-element.29.refs_0_), channel_id=1, source_target_pairs={{0,2},{1,3},{2,4},{3,5},{4,6},{5,7},{6,0},{7,1},{8,10},{9,11},{10,... | collective-permute-start | bytes 393224 | tf_op jit(solution)/shard_map/ppermute | solution.py:246
  65.3 20.2 %collective-permute-start.12 = (f32[128,256]{1,0:T(8,128)}, f32[128,256]{1,0:T(8,128)S(1)}, u32[]{:S(2)}, u32[]{:S(2)}) collective-permute-start(f32[128,256]{1,0:T(8,128)} %get-tuple-element.29.refs_0_), channel_id=1, source_target_pairs={{0,4},{1,5},{2,6},{3,7},{4,0},{5,1},{6,2},{7,3},{8,12},{9,13},{10,... | collective-permute-start | bytes 393224 | tf_op jit(solution)/shard_map/ppermute | solution.py:246
  69.1 16.4 %collective-permute-start.9 = (f32[128,256]{1,0:T(8,128)}, f32[128,256]{1,0:T(8,128)S(1)}, u32[]{:S(2)}, u32[]{:S(2)}) collective-permute-start(f32[128,256]{1,0:T(8,128)} %get-tuple-element.29.refs_0_), channel_id=1, source_target_pairs={{0,7},{1,0},{2,1},{3,2},{4,3},{5,4},{6,5},{7,6},{8,15},{9,8},{10,9... | collective-permute-start | bytes 393224 | tf_op jit(solution)/shard_map/ppermute | solution.py:246
  69.6 16.0 %collective-permute-start.8 = (f32[128,256]{1,0:T(8,128)}, f32[128,256]{1,0:T(8,128)S(1)}, u32[]{:S(2)}, u32[]{:S(2)}) collective-permute-start(f32[128,256]{1,0:T(8,128)} %get-tuple-element.29.refs_0_), channel_id=1, source_target_pairs={{0,1},{1,2},{2,3},{3,4},{4,5},{5,6},{6,7},{7,0},{8,9},{9,10},{10,1... | collective-permute-start | bytes 393224 | tf_op jit(solution)/shard_map/ppermute | solution.py:246
  70.7 27.4 %copy-start.7 = (f32[128,256]{1,0:T(8,128)}, f32[128,256]{1,0:T(8,128)S(1)}, u32[]{:S(2)}) copy-start(f32[128,256]{1,0:T(8,128)S(1)} %collective-permute-done.11.refs_4_) | copy-start | bytes 393220
  70.7 14.9 %collective-permute-start.14 = (f32[128,256]{1,0:T(8,128)S(1)}, f32[128,256]{1,0:T(8,128)S(1)}, u32[]{:S(2)}, u32[]{:S(2)}) collective-permute-start(f32[128,256]{1,0:T(8,128)S(1)} %collective-permute-done.11.refs_4_), channel_id=1, source_target_pairs={{0,7},{1,0},{2,1},{3,2},{4,3},{5,4},{6,5},{7,6},{8,15},{9,8},{10,9... | collective-permute-start | bytes 393224 | tf_op jit(solution)/shard_map/ppermute | solution.py:246
  74.1 24.0 %copy-start.8 = (f32[128,256]{1,0:T(8,128)}, f32[128,256]{1,0:T(8,128)S(1)}, u32[]{:S(2)}) copy-start(f32[128,256]{1,0:T(8,128)S(1)} %collective-permute-done.10.refs_3_) | copy-start | bytes 393220
  74.1 11.8 %collective-permute-start.13 = (f32[128,256]{1,0:T(8,128)S(1)}, f32[128,256]{1,0:T(8,128)S(1)}, u32[]{:S(2)}, u32[]{:S(2)}) collective-permute-start(f32[128,256]{1,0:T(8,128)S(1)} %collective-permute-done.10.refs_3_), channel_id=1, source_target_pairs={{0,1},{1,2},{2,3},{3,4},{4,5},{5,6},{6,7},{7,0},{8,9},{9,10},{10,1... | collective-permute-start | bytes 393224 | tf_op jit(solution)/shard_map/ppermute | solution.py:246
  85.6 12.5 %copy-start.10 = (f32[128,256]{1,0:T(8,128)}, f32[128,256]{1,0:T(8,128)S(1)}, u32[]{:S(2)}) copy-start(f32[128,256]{1,0:T(8,128)S(1)} %collective-permute-done.9.refs_2_) | copy-start | bytes 393220
  86.0 4.8 %collective-permute-start.15 = (f32[16,4,64,128]{3,2,1,0:T(8,128)S(1)}, f32[16,4,64,128]{3,2,1,0:T(8,128)}, u32[]{:S(2)}, u32[]{:S(2)}) collective-permute-start(f32[16,4,64,128]{3,2,1,0:T(8,128)S(1)} %all-to-all-done.1.refs_8_), channel_id=1, source_target_pairs={{0,8},{8,0},{16,24},{24,16},{32,40},{40,32},{48,56},{56,48},{64,72... | collective-permute-start | bytes 6291464 | tf_op jit(solution)/shard_map/ppermute | solution.py:300
  (8 other events, 75.5 us)

commit v4 on v3

--- a/solution.py
+++ b/solution.py
@@ -130,16 +130,22 @@
     cross[...] = times_rows(both, high[...], low[...])
 
 
-def child_kernel(ids, parents, widths, blocks, child_inv, *refs):
-    rows, sides, refs = refs[:8], refs[8:10], refs[10:]
-    image, below_high, below_low, base, lines = refs[:5]
-    factor, level1, panels, both, high, low, row_here, part_here = refs[5:]
+def child_kernel(ids, parents, widths, blocks, child_inv, root, *refs):
+    rows, sides, parts, refs = refs[:8], refs[8:10], refs[10:18], refs[18:]
+    payload, factor, level1, panels, cross, both, high, low = refs[:8]
+    row_here, part_here, cross_here = refs[8:]
+    cross_copies = [
+        pltpu.make_async_copy(
+            parts[n], cross.at[(ids[1] + 8 - away) % 8], cross_here.at[n]
+        )
+        for n, away in enumerate((0, 1, 7, 2, 6, 4, 3, 5))
+    ]
     copies = [
         pltpu.make_async_copy(side, panels.at[n], part_here.at[n])
         for n, side in enumerate(sides)
     ]
     row_copies = fetch_rows(ids, rows, factor, level1, row_here)
-    for copy in copies + row_copies:
+    for copy in copies + row_copies + cross_copies:
         copy.start()
     high[...] = jnp.zeros_like(high)
     low[...] = jnp.zeros_like(low)
@@ -159,14 +165,14 @@
                     high[pl.ds(row, 32), 128 * place : 128 * place + 128] = up
                     low[pl.ds(row, 32), 128 * place : 128 * place + 128] = down
     split_rows(row_copies, factor, both)
-    image[...] = times_rows(both, high[0:4096, :], low[0:4096, :])
-    below_high[...] = high[4096:5120, :]
-    below_low[...] = low[4096:5120, :]
-
+    image = times_rows(both, high[0:4096, :], low[0:4096, :])
+    below_high, below_low = high[4096:5120, :], low[4096:5120, :]
     depth = ids[2] * 32 + lax.broadcasted_iota(jnp.int32, (32, 128), 0)
+    ends = []
     for j in range(4):
         inside = jnp.logical_and(depth < widths[j], lanes < widths[j])
-        base[j : j + 1, :] = squares(jnp.where(inside, child_inv[j], 0.0))
+        ends.append(squares(jnp.where(inside, child_inv[j], 0.0)))
+    ends = jnp.concatenate(ends, axis=0)
     own = jnp.concatenate(
         [
             jnp.concatenate([level1[n, :, 128 * q : 128 * q + 128] for n in range(8)], axis=1)
@@ -174,51 +180,36 @@
         ],
         axis=0,
     )
-    lower = product(own, high[4096:5120, :], low[4096:5120, :])
+    lower = product(own, below_high, below_low)
     parity = lax.broadcasted_iota(jnp.int32, (64, 1024), 0) % 2
     parity_half = lax.broadcasted_iota(jnp.int32, (64, 256), 0) % 2
-    for which in range(2):
-        half = slice(256 * which, 256 * which + 256)
-        sums = squares(jnp.where(parity_half == which, lower[:, half], 0.0))
-        base[...] += by_child(parents, which, sums)
-        lines[which : which + 1, :] = squares(jnp.where(parity == which, own, 0.0))
-
-
-def by_child(parents, which, sums):
-    place = lax.broadcasted_iota(jnp.int32, (4, 128), 0)
-    first, second = kids_in_order(parents)[2 * which : 2 * which + 2]
-    return jnp.where(place == first, sums[:, :128], 0.0) + jnp.where(
-        place == second, sums[:, 128:], 0.0
-    )
-
-
-def finish_kernel(ids, parents, root, base, lines, image, below_high, below_low, *refs):
-    parts, (payload, cross, arrived) = refs[:8], refs[8:]
-    copies = []
-    for n, away in enumerate((0, 1, 7, 2, 6, 4, 3, 5)):
-        spot = cross.at[(ids[1] + 8 - away) % 8]
-        copies.append(pltpu.make_async_copy(parts[n], spot, arrived.at[n]))
-    for copy in copies:
-        copy.start()
-    for copy in copies:
+    for copy in cross_copies:
         copy.wait()
-    ends = base[...]
-    known_lines = []
+    lines = []
     for which in range(2):
         half = slice(256 * which, 256 * which + 256)
         known = jnp.concatenate(
             [cross[z, :, 128 * which : 128 * which + 128] for z in range(8)], axis=1
         )
         upper = image[:, half] - product(known, below_high[:, half], below_low[:, half])
-        ends = ends + by_child(parents, which, squares(upper))
-        known_lines.append(lines[which : which + 1, :] + squares(known))
+        sums = squares(upper) + squares(jnp.where(parity_half == which, lower[:, half], 0.0))
+        ends = ends + by_child(parents, which, sums)
+        lines.append(squares(known) + squares(jnp.where(parity == which, own, 0.0)))
     for i in range(32):
         b = i // 4
         payload[i, 0:4, :] = ends
         payload[i, 4:5, :] = root[b, :, 128 * (i % 4) : 128 * (i % 4) + 128]
-        payload[i, 5:6, :] = known_lines[0][:, 128 * b : 128 * b + 128]
-        payload[i, 6:7, :] = known_lines[1][:, 128 * b : 128 * b + 128]
+        payload[i, 5:6, :] = lines[0][:, 128 * b : 128 * b + 128]
+        payload[i, 6:7, :] = lines[1][:, 128 * b : 128 * b + 128]
         payload[i, 7:8, :] = jnp.zeros((1, 128), f32)
+
+
+def by_child(parents, which, sums):
+    place = lax.broadcasted_iota(jnp.int32, (4, 128), 0)
+    first, second = kids_in_order(parents)[2 * which : 2 * which + 2]
+    return jnp.where(place == first, sums[:, :128], 0.0) + jnp.where(
+        place == second, sums[:, 128:], 0.0
+    )
 
 
 def sum_kernel(ids, parts, root, parent, child):
@@ -299,32 +290,27 @@
     mine, _ = fence((mine, crosses))
     children = [mine, lax.ppermute(mine, "row", PAIRS)]
 
-    image, below_high, below_low, base, lines = call(
-        child_kernel,
-        [
-            ((128, 512), f32), ((1024, 512), bf16), ((1024, 512), bf16),
-            ((4, 128), f32), ((2, 1024), f32),
-        ],
-        [SMEM] * 4 + [VMEM] + [HBM] * 8 + [ANY, HBM], (1_600_000_000, 10_000_000),
+    (payload,) = call(
+        child_kernel, [((32, 8, 128), f32)],
+        [SMEM] * 4 + [VMEM] * 2 + [HBM] * 8 + [ANY, HBM] + [HBM] * 8,
+        (2_000_000_000, 10_000_000),
         [
             pltpu.VMEM((8, 128, 512), f32),
             pltpu.VMEM((8, 16, 512), f32),
             pltpu.VMEM((2, 16, 4, 64, 128), f32),
+            pltpu.VMEM((8, 128, 256), f32),
             pltpu.VMEM((256, 4096), bf16),
             pltpu.VMEM((5120, 512), bf16),
             pltpu.VMEM((5120, 512), bf16),
             pltpu.SemaphoreType.DMA((16,)),
             pltpu.SemaphoreType.DMA((2,)),
+            pltpu.SemaphoreType.DMA((8,)),
         ],
-        30,
-    )(ids, child_parent, child_width, child_blocks, child_inv, *rows, *children)
-
-    (payload,) = call(
-        finish_kernel, [((32, 8, 128), f32)], [SMEM] * 2 + [VMEM] * 6 + [ANY] * 8,
-        (500_000_000, 3_000_000),
-        [pltpu.VMEM((8, 128, 256), f32), pltpu.SemaphoreType.DMA((8,))],
-        16,
-    )(ids, child_parent, root, base, lines, image, below_high, below_low, *crosses)
+        60,
+    )(
+        ids, child_parent, child_width, child_blocks, child_inv, root,
+        *rows, *children, *crosses,
+    )
     root, parent, child = call(
         sum_kernel, [((1, 128), f32), ((2, 32), f32), ((4, 128), f32)], [SMEM, VMEM],
         (0, 130_000), (), 16,

time: 117 us -> 115 us (0.983)
  Pallas kernels: 21.9 us -> 18.5 us
  local copies, waits for them, and re-layouts: 0.76 us -> 2.1 us
    pallas_call x2 -> x1, Pallas kernels: 11.6 us -> 8.15 us  [body(): call(child_kernel, [((32, 8, 128), f32)], [SMEM] * 4 + [VMEM] * 2 + [HBM]...]
    unnamed x28 -> x30, local copies, waits for them, and re-layouts: 0.76 us -> 2.1 us
  transfers between devices with their start and end apart: 18 -> 18, of which waited for: 11 -> 11; matrix products, arithmetic and copies ran while one was open for 1% -> 1% of each run, Pallas kernels for 4% -> 5%
where the time goes in v4:
time: 115 us; the launch traced here: 114 us
  starting transfers between devices  41.2 us (36%)
  waiting for transfers between devices  38.7 us (34%)
  Pallas kernels  18.5 us (16%)
  blocking collectives  12.3 us (11%)
  local copies, waits for them, and re-layouts  2.1 us (2%)
    ppermute x14, starting transfers between devices, along(): return lax.ppermute(x, 'col', [(z, (z + n) % 8) for z in range(8)])  24.2 us
    ppermute x14, waiting for transfers between devices, along(): return lax.ppermute(x, 'col', [(z, (z + n) % 8) for z in range(8)])  22.5 us
    all_to_all x1, blocking collectives, body(): lax.all_to_all(payload, 'row', 0, 0, tiled=True)  12.3 us
    all_to_all x1, waiting for transfers between devices, body(): lax.all_to_all(children, 'row', 0, 0, tiled=True, axis_index_groups=SAME_...  11.4 us
    pallas_call x1, Pallas kernels, body(): call(child_kernel, [((32, 8, 128), f32)], [SMEM] * 4 + [VMEM] * 2 + [HBM]...  8.15 us
    all_to_all x1, starting transfers between devices, body(): lax.all_to_all(panels, 'row', 0, 0, tiled=True, axis_index_groups=SAME_CORE)  7.77 us
    all_to_all x1, starting transfers between devices, body(): lax.all_to_all(children, 'row', 0, 0, tiled=True, axis_index_groups=SAME_...  5.42 us
    pallas_call x1, Pallas kernels, body(): call(cross_kernel, [((128, 256), f32), ((8, 1, 512), f32)], [SMEM] + [HBM...  5.17 us
  transfers between devices with their start and end apart: 18, of which 11 were waited for; matrix products, arithmetic and copies ran while one was open for 1% of the time, Pallas kernels for 5%

profile of v4, /device:TPU:1, one launch (start us, length us, event | category | flops | bytes accessed | tf_op | source)
XLA Modules:
  0.0 114.2 jit_solution(17719643857892257062)
XLA Ops:
  0.6 3.4 %shard_map.103 = (f32[144,512]{1,0:T(8,128)}, f32[16,2,128,128]{3,2,1,0:T(8,128)}, f32[16,4,64,128]{3,2,1,0:T(8,128)}) custom-call(f32[128,512]{1,0:T(8,128)} %root_inv.1, f32[64,128]{1,0:T(8,128)} %bitcast.7, f32[256,128]{1,0:T(8,128)} %bitcast.6, f32[4,64,128]{2,1,0:T(8,128)} %child.1), custom_call_target="tpu_custom_call" | custom-call | bytes 5000000 | tf_op jit(solution)/shard_map/pallas_call | solution.py:254
  4.0 7.8 %all-to-all-start = ((f32[16,2,128,128]{3,2,1,0:T(8,128)}), f32[16,2,128,128]{3,2,1,0:T(8,128)}, u32[]{:S(2)}, u32[]{:S(2)}) async-start(f32[16,2,128,128]{3,2,1,0:T(8,128)} %get-tuple-element.17), calls=%async_computation | async-start | bytes 4194304 | tf_op jit(solution)/shard_map/all_to_all | solution.py:264
  11.8 5.7 %collective-permute-start.3 = (f32[144,512]{1,0:T(8,128)S(1)}, f32[144,512]{1,0:T(8,128)S(1)}, u32[]{:S(2)}, u32[]{:S(2)}) collective-permute-start(f32[144,512]{1,0:T(8,128)S(1)} %copy-done.2), channel_id=1, source_target_pairs={{0,7},{1,0},{2,1},{3,2},{4,3},{5,4},{6,5},{7,6},{8,15},{9,8},{10,9... | collective-permute-start | bytes 884744 | tf_op jit(solution)/shard_map/ppermute | solution.py:237
  17.4 5.4 %collective-permute-done.3.refs_5_ = f32[144,512]{1,0:T(8,128)S(1)} collective-permute-done((f32[144,512]{1,0:T(8,128)S(1)}, f32[144,512]{1,0:T(8,128)S(1)}, u32[]{:S(2)}, u32[]{:S(2)}) %collective-permute-start.3) | collective-permute-done | bytes 294944 | tf_op jit(solution)/shard_map/ppermute | solution.py:237
  22.8 3.5 %collective-permute-start.4 = (f32[144,512]{1,0:T(8,128)S(1)}, f32[144,512]{1,0:T(8,128)S(1)}, u32[]{:S(2)}, u32[]{:S(2)}) collective-permute-start(f32[144,512]{1,0:T(8,128)S(1)} %collective-permute-done.3.refs_5_), channel_id=1, source_target_pairs={{0,7},{1,0},{2,1},{3,2},{4,3},{5,4},{6,5},{7,6},{8,15},{9,8},{10,9... | collective-permute-start | bytes 884744 | tf_op jit(solution)/shard_map/ppermute | solution.py:237
  26.3 4.5 %collective-permute-done.4.refs_6_ = f32[144,512]{1,0:T(8,128)S(1)} collective-permute-done((f32[144,512]{1,0:T(8,128)S(1)}, f32[144,512]{1,0:T(8,128)S(1)}, u32[]{:S(2)}, u32[]{:S(2)}) %collective-permute-start.4) | collective-permute-done | bytes 294944 | tf_op jit(solution)/shard_map/ppermute | solution.py:237
  30.9 3.5 %collective-permute-start.5 = (f32[144,512]{1,0:T(8,128)S(1)}, f32[144,512]{1,0:T(8,128)S(1)}, u32[]{:S(2)}, u32[]{:S(2)}) collective-permute-start(f32[144,512]{1,0:T(8,128)S(1)} %collective-permute-done.4.refs_6_), channel_id=1, source_target_pairs={{0,7},{1,0},{2,1},{3,2},{4,3},{5,4},{6,5},{7,6},{8,15},{9,8},{10,9... | collective-permute-start | bytes 884744 | tf_op jit(solution)/shard_map/ppermute | solution.py:237
  34.4 3.7 %collective-permute-done.5.refs_7_ = f32[144,512]{1,0:T(8,128)S(1)} collective-permute-done((f32[144,512]{1,0:T(8,128)S(1)}, f32[144,512]{1,0:T(8,128)S(1)}, u32[]{:S(2)}, u32[]{:S(2)}) %collective-permute-start.5) | collective-permute-done | bytes 294944 | tf_op jit(solution)/shard_map/ppermute | solution.py:237
  38.8 2.5 %collective-permute-done.2.refs_3_ = f32[144,512]{1,0:T(8,128)} collective-permute-done((f32[144,512]{1,0:T(8,128)S(1)}, f32[144,512]{1,0:T(8,128)}, u32[]{:S(2)}, u32[]{:S(2)}) %collective-permute-start.2) | collective-permute-done | bytes 294944 | tf_op jit(solution)/shard_map/ppermute | solution.py:237
  41.3 1.0 all-to-all-done.refs_8_
  42.3 3.0 %collective-permute-start.7 = (f32[16,2,128,128]{3,2,1,0:T(8,128)}, f32[16,2,128,128]{3,2,1,0:T(8,128)}, u32[]{:S(2)}, u32[]{:S(2)}) collective-permute-start(f32[16,2,128,128]{3,2,1,0:T(8,128)} %all-to-all-done.refs_8_), channel_id=1, source_target_pairs={{0,8},{8,0},{16,24},{24,16},{32,40},{40,32},{48,56},{56,48},{64,72... | collective-permute-start | bytes 6291464 | tf_op jit(solution)/shard_map/ppermute | solution.py:269
  46.7 5.4 %all-to-all-start.1 = ((f32[16,4,64,128]{3,2,1,0:T(8,128)}), f32[16,4,64,128]{3,2,1,0:T(8,128)S(1)}, u32[]{:S(2)}, u32[]{:S(2)}) async-start(f32[16,4,64,128]{3,2,1,0:T(8,128)} %get-tuple-element.23), calls=%async_computation.1 | async-start | bytes 4194304 | tf_op jit(solution)/shard_map/all_to_all | solution.py:270
  52.2 5.6 %collective-permute-done.6.refs_4_ = f32[144,512]{1,0:T(8,128)} collective-permute-done((f32[144,512]{1,0:T(8,128)}, f32[144,512]{1,0:T(8,128)}, u32[]{:S(2)}, u32[]{:S(2)}) %collective-permute-start.6) | collective-permute-done | bytes 294944 | tf_op jit(solution)/shard_map/ppermute | solution.py:237
  57.7 5.2 %shard_map.104 = (f32[128,256]{1,0:T(8,128)}, f32[8,1,512]{2,1,0:T(1,128)}) custom-call(s32[3]{0:T(128)} %pad_add_fusion.ids, f32[144,512]{1,0:T(8,128)} %get-tuple-element.16.refs_0_, f32[144,512]{1,0:T(8,128)} %copy-done.4, f32[144,512]{1,0:T(8,128)} %copy-done.6, f32[144,512]{1,0:T(8,128)} %collective-permute-done.2.refs_3_, ...), custom_call_target="tpu_custom_call" | custom-call | flops 40000000000 | bytes 6000000 | tf_op jit(solution)/shard_map/pallas_call | solution.py:274
  62.9 1.8 %collective-permute-start.11 = (f32[128,256]{1,0:T(8,128)}, f32[128,256]{1,0:T(8,128)S(1)}, u32[]{:S(2)}, u32[]{:S(2)}) collective-permute-start(f32[128,256]{1,0:T(8,128)} %get-tuple-element.24.refs_10_), channel_id=1, source_target_pairs={{0,6},{1,7},{2,0},{3,1},{4,2},{5,3},{6,4},{7,5},{8,14},{9,15},{10,... | collective-permute-start | bytes 393224 | tf_op jit(solution)/shard_map/ppermute | solution.py:237
  65.3 3.8 %collective-permute-start.12 = (f32[128,256]{1,0:T(8,128)}, f32[128,256]{1,0:T(8,128)S(1)}, u32[]{:S(2)}, u32[]{:S(2)}) collective-permute-start(f32[128,256]{1,0:T(8,128)} %get-tuple-element.24.refs_10_), channel_id=1, source_target_pairs={{0,4},{1,5},{2,6},{3,7},{4,0},{5,1},{6,2},{7,3},{8,12},{9,13},{10,... | collective-permute-start | bytes 393224 | tf_op jit(solution)/shard_map/ppermute | solution.py:237
  69.6 1.0 collective-permute-start.8
  70.7 3.0 %collective-permute-start.14 = (f32[128,256]{1,0:T(8,128)S(1)}, f32[128,256]{1,0:T(8,128)S(1)}, u32[]{:S(2)}, u32[]{:S(2)}) collective-permute-start(f32[128,256]{1,0:T(8,128)S(1)} %collective-permute-done.11.refs_14_), channel_id=1, source_target_pairs={{0,7},{1,0},{2,1},{3,2},{4,3},{5,4},{6,5},{7,6},{8,15},{9,8},{10,9... | collective-permute-start | bytes 393224 | tf_op jit(solution)/shard_map/ppermute | solution.py:237
  74.1 11.4 %all-to-all-done.1.refs_8_ = f32[16,4,64,128]{3,2,1,0:T(8,128)S(1)} async-done(((f32[16,4,64,128]{3,2,1,0:T(8,128)}), f32[16,4,64,128]{3,2,1,0:T(8,128)S(1)}, u32[]{:S(2)}, u32[]{:S(2)}) %all-to-all-start.1) | async-done | bytes 2097184 | tf_op jit(solution)/shard_map/all_to_all | solution.py:270
  86.8 3.8 %collective-permute-done.15.refs_9_ = f32[16,4,64,128]{3,2,1,0:T(8,128)S(1)} collective-permute-done((f32[16,4,64,128]{3,2,1,0:T(8,128)S(1)}, f32[16,4,64,128]{3,2,1,0:T(8,128)S(1)}, u32[]{:S(2)}, u32[]{:S(2)}) %collective-permute-start.15) | collective-permute-done | bytes 2097184 | tf_op jit(solution)/shard_map/ppermute | solution.py:291
  90.6 1.3 %copy-done.1 = f32[16,4,64,128]{3,2,1,0:T(8,128)} copy-done((f32[16,4,64,128]{3,2,1,0:T(8,128)}, f32[16,4,64,128]{3,2,1,0:T(8,128)S(1)}, u32[]{:S(2)}) %copy-start.1) | copy-done | bytes 2097176
  92.0 8.1 %shard_map.105 = f32[32,8,128]{2,1,0:T(8,128)} custom-call(s32[3]{0:T(128)} %pad_add_fusion.ids, s32[4]{0:T(128)} %parents.1, s32[4]{0:T(128)} %widths.1, s32[4,64]{1,0:T(4,128)} %blocks.1, f32[4,32,128]{2,1,0:T(8,128)} %child_inv.1, f32[8,1,512]{2,1,0:T(1,128)} %get-tuple-element.22.root, f32[144,512]{1,0:T(8,128)} %get-tuple-element.16.refs_0_, ...), custom_call_target="tpu_custom_call" | custom-call | flops 2000000000 | bytes 10000000 | tf_op jit(solution)/shard_map/pallas_call | solution.py:293
  100.2 12.3 %all_to_all.15.parts = f32[32,8,128]{2,1,0:T(8,128)} all-to-all(f32[32,8,128]{2,1,0:T(8,128)} %shard_map.105), channel_id=1, replica_groups=mesh['row'=32,'col'=8] {'row'}, dimensions={0} | all-to-all | bytes 262144 | tf_op jit(solution)/shard_map/all_to_all | solution.py:317
  112.4 1.8 %shard_map.106 = (f32[1,128]{1,0:T(1,128)}, f32[2,32]{1,0:T(2,128)}, f32[4,128]{1,0:T(4,128)}) custom-call(s32[3]{0:T(128)} %pad_add_fusion.ids, f32[32,8,128]{2,1,0:T(8,128)} %all_to_all.15.parts), custom_call_target="tpu_custom_call" | custom-call | bytes 130000 | tf_op jit(solution)/shard_map/pallas_call | solution.py:314
  (48 shorter events, 5.1 us)
Async XLA Ops:
  4.0 38.3 %all-to-all-start = ((f32[16,2,128,128]{3,2,1,0:T(8,128)}), f32[16,2,128,128]{3,2,1,0:T(8,128)}, u32[]{:S(2)}, u32[]{:S(2)}) async-start(f32[16,2,128,128]{3,2,1,0:T(8,128)} %get-tuple-element.17), calls=%async_computation | async-start | bytes 4194304 | tf_op jit(solution)/shard_map/all_to_all | solution.py:264
  11.8 11.0 %collective-permute-start.3 = (f32[144,512]{1,0:T(8,128)S(1)}, f32[144,512]{1,0:T(8,128)S(1)}, u32[]{:S(2)}, u32[]{:S(2)}) collective-permute-start(f32[144,512]{1,0:T(8,128)S(1)} %copy-done.2), channel_id=1, source_target_pairs={{0,7},{1,0},{2,1},{3,2},{4,3},{5,4},{6,5},{7,6},{8,15},{9,8},{10,9... | collective-permute-start | bytes 884744 | tf_op jit(solution)/shard_map/ppermute | solution.py:237
  17.4 8.9 %collective-permute-start = (f32[144,512]{1,0:T(8,128)S(1)}, f32[144,512]{1,0:T(8,128)S(1)}, u32[]{:S(2)}, u32[]{:S(2)}) collective-permute-start(f32[144,512]{1,0:T(8,128)S(1)} %copy-done.2), channel_id=1, source_target_pairs={{0,1},{1,2},{2,3},{3,4},{4,5},{5,6},{6,7},{7,0},{8,9},{9,10},{10,1... | collective-permute-start | bytes 884744 | tf_op jit(solution)/shard_map/ppermute | solution.py:237
  22.8 23.9 %copy-start.3 = (f32[144,512]{1,0:T(8,128)}, f32[144,512]{1,0:T(8,128)S(1)}, u32[]{:S(2)}) copy-start(f32[144,512]{1,0:T(8,128)S(1)} %collective-permute-done.3.refs_5_) | copy-start | bytes 884740
  22.8 8.1 %collective-permute-start.4 = (f32[144,512]{1,0:T(8,128)S(1)}, f32[144,512]{1,0:T(8,128)S(1)}, u32[]{:S(2)}, u32[]{:S(2)}) collective-permute-start(f32[144,512]{1,0:T(8,128)S(1)} %collective-permute-done.3.refs_5_), channel_id=1, source_target_pairs={{0,7},{1,0},{2,1},{3,2},{4,3},{5,4},{6,5},{7,6},{8,15},{9,8},{10,9... | collective-permute-start | bytes 884744 | tf_op jit(solution)/shard_map/ppermute | solution.py:237
  26.3 20.4 %copy-start.4 = (f32[144,512]{1,0:T(8,128)}, f32[144,512]{1,0:T(8,128)S(1)}, u32[]{:S(2)}) copy-start(f32[144,512]{1,0:T(8,128)S(1)} %collective-permute-done.refs_1_) | copy-start | bytes 884740
  26.3 8.1 %collective-permute-start.1 = (f32[144,512]{1,0:T(8,128)S(1)}, f32[144,512]{1,0:T(8,128)S(1)}, u32[]{:S(2)}, u32[]{:S(2)}) collective-permute-start(f32[144,512]{1,0:T(8,128)S(1)} %collective-permute-done.refs_1_), channel_id=1, source_target_pairs={{0,1},{1,2},{2,3},{3,4},{4,5},{5,6},{6,7},{7,0},{8,9},{9,10},{10,1... | collective-permute-start | bytes 884744 | tf_op jit(solution)/shard_map/ppermute | solution.py:237
  30.9 15.9 %copy-start.5 = (f32[144,512]{1,0:T(8,128)}, f32[144,512]{1,0:T(8,128)S(1)}, u32[]{:S(2)}) copy-start(f32[144,512]{1,0:T(8,128)S(1)} %collective-permute-done.4.refs_6_) | copy-start | bytes 884740
  30.9 7.2 %collective-permute-start.5 = (f32[144,512]{1,0:T(8,128)S(1)}, f32[144,512]{1,0:T(8,128)S(1)}, u32[]{:S(2)}, u32[]{:S(2)}) collective-permute-start(f32[144,512]{1,0:T(8,128)S(1)} %collective-permute-done.4.refs_6_), channel_id=1, source_target_pairs={{0,7},{1,0},{2,1},{3,2},{4,3},{5,4},{6,5},{7,6},{8,15},{9,8},{10,9... | collective-permute-start | bytes 884744 | tf_op jit(solution)/shard_map/ppermute | solution.py:237
  34.4 12.3 %copy-start.6 = (f32[144,512]{1,0:T(8,128)}, f32[144,512]{1,0:T(8,128)S(1)}, u32[]{:S(2)}) copy-start(f32[144,512]{1,0:T(8,128)S(1)} %collective-permute-done.1.refs_2_) | copy-start | bytes 884740
  34.4 6.9 %collective-permute-start.2 = (f32[144,512]{1,0:T(8,128)S(1)}, f32[144,512]{1,0:T(8,128)}, u32[]{:S(2)}, u32[]{:S(2)}) collective-permute-start(f32[144,512]{1,0:T(8,128)S(1)} %collective-permute-done.1.refs_2_), channel_id=1, source_target_pairs={{0,1},{1,2},{2,3},{3,4},{4,5},{5,6},{6,7},{7,0},{8,9},{9,10},{10,1... | collective-permute-start | bytes 884744 | tf_op jit(solution)/shard_map/ppermute | solution.py:237
  42.3 15.4 %collective-permute-start.7 = (f32[16,2,128,128]{3,2,1,0:T(8,128)}, f32[16,2,128,128]{3,2,1,0:T(8,128)}, u32[]{:S(2)}, u32[]{:S(2)}) collective-permute-start(f32[16,2,128,128]{3,2,1,0:T(8,128)} %all-to-all-done.refs_8_), channel_id=1, source_target_pairs={{0,8},{8,0},{16,24},{24,16},{32,40},{40,32},{48,56},{56,48},{64,72... | collective-permute-start | bytes 6291464 | tf_op jit(solution)/shard_map/ppermute | solution.py:269
  45.3 12.4 %collective-permute-start.6 = (f32[144,512]{1,0:T(8,128)}, f32[144,512]{1,0:T(8,128)}, u32[]{:S(2)}, u32[]{:S(2)}) collective-permute-start(f32[144,512]{1,0:T(8,128)} %collective-permute-done.2.refs_3_), channel_id=1, source_target_pairs={{0,1},{1,2},{2,3},{3,4},{4,5},{5,6},{6,7},{7,0},{8,9},{9,10},{10,1... | collective-permute-start | bytes 884744 | tf_op jit(solution)/shard_map/ppermute | solution.py:237
  46.7 38.8 %all-to-all-start.1 = ((f32[16,4,64,128]{3,2,1,0:T(8,128)}), f32[16,4,64,128]{3,2,1,0:T(8,128)S(1)}, u32[]{:S(2)}, u32[]{:S(2)}) async-start(f32[16,4,64,128]{3,2,1,0:T(8,128)} %get-tuple-element.23), calls=%async_computation.1 | async-start | bytes 4194304 | tf_op jit(solution)/shard_map/all_to_all | solution.py:270
  62.9 7.8 %collective-permute-start.11 = (f32[128,256]{1,0:T(8,128)}, f32[128,256]{1,0:T(8,128)S(1)}, u32[]{:S(2)}, u32[]{:S(2)}) collective-permute-start(f32[128,256]{1,0:T(8,128)} %get-tuple-element.24.refs_10_), channel_id=1, source_target_pairs={{0,6},{1,7},{2,0},{3,1},{4,2},{5,3},{6,4},{7,5},{8,14},{9,15},{10,... | collective-permute-start | bytes 393224 | tf_op jit(solution)/shard_map/ppermute | solution.py:237
  64.7 9.4 %collective-permute-start.10 = (f32[128,256]{1,0:T(8,128)}, f32[128,256]{1,0:T(8,128)S(1)}, u32[]{:S(2)}, u32[]{:S(2)}) collective-permute-start(f32[128,256]{1,0:T(8,128)} %get-tuple-element.24.refs_10_), channel_id=1, source_target_pairs={{0,2},{1,3},{2,4},{3,5},{4,6},{5,7},{6,0},{7,1},{8,10},{9,11},{10,... | collective-permute-start | bytes 393224 | tf_op jit(solution)/shard_map/ppermute | solution.py:237
  65.3 20.2 %collective-permute-start.12 = (f32[128,256]{1,0:T(8,128)}, f32[128,256]{1,0:T(8,128)S(1)}, u32[]{:S(2)}, u32[]{:S(2)}) collective-permute-start(f32[128,256]{1,0:T(8,128)} %get-tuple-element.24.refs_10_), channel_id=1, source_target_pairs={{0,4},{1,5},{2,6},{3,7},{4,0},{5,1},{6,2},{7,3},{8,12},{9,13},{10,... | collective-permute-start | bytes 393224 | tf_op jit(solution)/shard_map/ppermute | solution.py:237
  69.1 16.4 %collective-permute-start.9 = (f32[128,256]{1,0:T(8,128)}, f32[128,256]{1,0:T(8,128)S(1)}, u32[]{:S(2)}, u32[]{:S(2)}) collective-permute-start(f32[128,256]{1,0:T(8,128)} %get-tuple-element.24.refs_10_), channel_id=1, source_target_pairs={{0,7},{1,0},{2,1},{3,2},{4,3},{5,4},{6,5},{7,6},{8,15},{9,8},{10,9... | collective-permute-start | bytes 393224 | tf_op jit(solution)/shard_map/ppermute | solution.py:237
  69.6 16.0 %collective-permute-start.8 = (f32[128,256]{1,0:T(8,128)}, f32[128,256]{1,0:T(8,128)S(1)}, u32[]{:S(2)}, u32[]{:S(2)}) collective-permute-start(f32[128,256]{1,0:T(8,128)} %get-tuple-element.24.refs_10_), channel_id=1, source_target_pairs={{0,1},{1,2},{2,3},{3,4},{4,5},{5,6},{6,7},{7,0},{8,9},{9,10},{10,1... | collective-permute-start | bytes 393224 | tf_op jit(solution)/shard_map/ppermute | solution.py:237
  70.7 21.3 %copy-start.8 = (f32[128,256]{1,0:T(8,128)}, f32[128,256]{1,0:T(8,128)S(1)}, u32[]{:S(2)}) copy-start(f32[128,256]{1,0:T(8,128)S(1)} %collective-permute-done.11.refs_14_) | copy-start | bytes 393220
  70.7 14.9 %collective-permute-start.14 = (f32[128,256]{1,0:T(8,128)S(1)}, f32[128,256]{1,0:T(8,128)S(1)}, u32[]{:S(2)}, u32[]{:S(2)}) collective-permute-start(f32[128,256]{1,0:T(8,128)S(1)} %collective-permute-done.11.refs_14_), channel_id=1, source_target_pairs={{0,7},{1,0},{2,1},{3,2},{4,3},{5,4},{6,5},{7,6},{8,15},{9,8},{10,9... | collective-permute-start | bytes 393224 | tf_op jit(solution)/shard_map/ppermute | solution.py:237
  74.1 17.8 %copy-start.9 = (f32[128,256]{1,0:T(8,128)}, f32[128,256]{1,0:T(8,128)S(1)}, u32[]{:S(2)}) copy-start(f32[128,256]{1,0:T(8,128)S(1)} %collective-permute-done.10.refs_13_) | copy-start | bytes 393220
  74.1 11.8 %collective-permute-start.13 = (f32[128,256]{1,0:T(8,128)S(1)}, f32[128,256]{1,0:T(8,128)S(1)}, u32[]{:S(2)}, u32[]{:S(2)}) collective-permute-start(f32[128,256]{1,0:T(8,128)S(1)} %collective-permute-done.10.refs_13_), channel_id=1, source_target_pairs={{0,1},{1,2},{2,3},{3,4},{4,5},{5,6},{6,7},{7,0},{8,9},{9,10},{10,1... | collective-permute-start | bytes 393224 | tf_op jit(solution)/shard_map/ppermute | solution.py:237
  86.0 4.7 %collective-permute-start.15 = (f32[16,4,64,128]{3,2,1,0:T(8,128)S(1)}, f32[16,4,64,128]{3,2,1,0:T(8,128)S(1)}, u32[]{:S(2)}, u32[]{:S(2)}) collective-permute-start(f32[16,4,64,128]{3,2,1,0:T(8,128)S(1)} %all-to-all-done.1.refs_8_), channel_id=1, source_target_pairs={{0,8},{8,0},{16,24},{24,16},{32,40},{40,32},{48,56},{56,48},{64,72... | collective-permute-start | bytes 6291464 | tf_op jit(solution)/shard_map/ppermute | solution.py:291
  (9 other events, 47.9 us)

commit v5 on v4

--- a/solution.py
+++ b/solution.py
@@ -141,8 +141,7 @@
         for n, away in enumerate((0, 1, 7, 2, 6, 4, 3, 5))
     ]
     copies = [
-        pltpu.make_async_copy(side, panels.at[n], part_here.at[n])
-        for n, side in enumerate(sides)
+        pltpu.make_async_copy(sides[0], panels, part_here.at[0])
     ]
     row_copies = fetch_rows(ids, rows, factor, level1, row_here)
     for copy in copies + row_copies + cross_copies:
@@ -152,15 +151,16 @@
     lanes = ids[1] * 128 + lax.broadcasted_iota(jnp.int32, (32, 128), 1)
     order = kids_in_order(parents)
     live = [lanes < widths[kid] for kid in order]
-    for n, copy in enumerate(copies):
-        copy.wait()
+    for n, side in enumerate((panels, sides[1])):
+        if n == 0:
+            copies[0].wait()
         core = ids[0] if n == 0 else 1 - ids[0]
         for chip in range(16):
             for half in range(2):
                 slot = 4 * chip + 2 * core + half
                 for place, kid in enumerate(order):
                     row = pl.multiple_of(blocks[kid, slot] * BLOCK_ROWS, BLOCK_ROWS)
-                    piece = panels[n, chip, kid, 32 * half : 32 * half + 32, :]
+                    piece = side[chip, kid, 32 * half : 32 * half + 32, :]
                     up, down = split(jnp.where(live[place], piece, 0.0))
                     high[pl.ds(row, 32), 128 * place : 128 * place + 128] = up
                     low[pl.ds(row, 32), 128 * place : 128 * place + 128] = down
@@ -292,21 +292,21 @@
 
     (payload,) = call(
         child_kernel, [((32, 8, 128), f32)],
-        [SMEM] * 4 + [VMEM] * 2 + [HBM] * 8 + [ANY, HBM] + [HBM] * 8,
+        [SMEM] * 4 + [VMEM] * 2 + [HBM] * 8 + [ANY, VMEM] + [HBM] * 8,
         (2_000_000_000, 10_000_000),
         [
             pltpu.VMEM((8, 128, 512), f32),
             pltpu.VMEM((8, 16, 512), f32),
-            pltpu.VMEM((2, 16, 4, 64, 128), f32),
+            pltpu.VMEM((16, 4, 64, 128), f32),
             pltpu.VMEM((8, 128, 256), f32),
             pltpu.VMEM((256, 4096), bf16),
             pltpu.VMEM((5120, 512), bf16),
             pltpu.VMEM((5120, 512), bf16),
             pltpu.SemaphoreType.DMA((16,)),
-            pltpu.SemaphoreType.DMA((2,)),
+            pltpu.SemaphoreType.DMA((1,)),
             pltpu.SemaphoreType.DMA((8,)),
         ],
-        60,
+        28,
     )(
         ids, child_parent, child_width, child_blocks, child_inv, root,
         *rows, *children, *crosses,

time: 115 us -> 115 us (level)
  no operation moved by 1% of the time
where the time goes in v5:
time: 115 us
  starting transfers between devices  41.2 us (36%)
  waiting for transfers between devices  38.7 us (34%)
  Pallas kernels  19 us (17%)
  blocking collectives  12.3 us (11%)
  local copies, waits for them, and re-layouts  2.1 us (2%)
    ppermute x14, starting transfers between devices, along(): return lax.ppermute(x, 'col', [(z, (z + n) % 8) for z in range(8)])  24.2 us
    ppermute x14, waiting for transfers between devices, along(): return lax.ppermute(x, 'col', [(z, (z + n) % 8) for z in range(8)])  22.5 us
    all_to_all x1, blocking collectives, body(): lax.all_to_all(payload, 'row', 0, 0, tiled=True)  12.3 us
    all_to_all x1, waiting for transfers between devices, body(): lax.all_to_all(children, 'row', 0, 0, tiled=True, axis_index_groups=SAME_...  11.4 us
    pallas_call x1, Pallas kernels, body(): call(child_kernel, [((32, 8, 128), f32)], [SMEM] * 4 + [VMEM] * 2 + [HBM]...  8.64 us
    all_to_all x1, starting transfers between devices, body(): lax.all_to_all(panels, 'row', 0, 0, tiled=True, axis_index_groups=SAME_CORE)  7.77 us
    all_to_all x1, starting transfers between devices, body(): lax.all_to_all(children, 'row', 0, 0, tiled=True, axis_index_groups=SAME_...  5.42 us
    pallas_call x1, Pallas kernels, body(): call(cross_kernel, [((128, 256), f32), ((8, 1, 512), f32)], [SMEM] + [HBM...  5.17 us
  transfers between devices with their start and end apart: 18, of which 11 were waited for; matrix products, arithmetic and copies ran while one was open for 1% of the time, Pallas kernels for 5%

profile of v5, /device:TPU:1, one launch (start us, length us, event | category | flops | bytes accessed | tf_op | source)
XLA Modules:
  0.0 114.7 jit_solution(7949299359507169019)
XLA Ops:
  0.6 3.4 %shard_map.103 = (f32[144,512]{1,0:T(8,128)}, f32[16,2,128,128]{3,2,1,0:T(8,128)}, f32[16,4,64,128]{3,2,1,0:T(8,128)}) custom-call(f32[128,512]{1,0:T(8,128)} %root_inv.1, f32[64,128]{1,0:T(8,128)} %bitcast.7, f32[256,128]{1,0:T(8,128)} %bitcast.6, f32[4,64,128]{2,1,0:T(8,128)} %child.1), custom_call_target="tpu_custom_call" | custom-call | bytes 5000000 | tf_op jit(solution)/shard_map/pallas_call | solution.py:254
  4.0 7.8 %all-to-all-start = ((f32[16,2,128,128]{3,2,1,0:T(8,128)}), f32[16,2,128,128]{3,2,1,0:T(8,128)}, u32[]{:S(2)}, u32[]{:S(2)}) async-start(f32[16,2,128,128]{3,2,1,0:T(8,128)} %get-tuple-element.17), calls=%async_computation | async-start | bytes 4194304 | tf_op jit(solution)/shard_map/all_to_all | solution.py:264
  11.8 5.7 %collective-permute-start.3 = (f32[144,512]{1,0:T(8,128)S(1)}, f32[144,512]{1,0:T(8,128)S(1)}, u32[]{:S(2)}, u32[]{:S(2)}) collective-permute-start(f32[144,512]{1,0:T(8,128)S(1)} %copy-done.2), channel_id=1, source_target_pairs={{0,7},{1,0},{2,1},{3,2},{4,3},{5,4},{6,5},{7,6},{8,15},{9,8},{10,9... | collective-permute-start | bytes 884744 | tf_op jit(solution)/shard_map/ppermute | solution.py:237
  17.4 5.4 %collective-permute-done.3.refs_5_ = f32[144,512]{1,0:T(8,128)S(1)} collective-permute-done((f32[144,512]{1,0:T(8,128)S(1)}, f32[144,512]{1,0:T(8,128)S(1)}, u32[]{:S(2)}, u32[]{:S(2)}) %collective-permute-start.3) | collective-permute-done | bytes 294944 | tf_op jit(solution)/shard_map/ppermute | solution.py:237
  22.8 3.5 %collective-permute-start.4 = (f32[144,512]{1,0:T(8,128)S(1)}, f32[144,512]{1,0:T(8,128)S(1)}, u32[]{:S(2)}, u32[]{:S(2)}) collective-permute-start(f32[144,512]{1,0:T(8,128)S(1)} %collective-permute-done.3.refs_5_), channel_id=1, source_target_pairs={{0,7},{1,0},{2,1},{3,2},{4,3},{5,4},{6,5},{7,6},{8,15},{9,8},{10,9... | collective-permute-start | bytes 884744 | tf_op jit(solution)/shard_map/ppermute | solution.py:237
  26.3 4.5 %collective-permute-done.4.refs_6_ = f32[144,512]{1,0:T(8,128)S(1)} collective-permute-done((f32[144,512]{1,0:T(8,128)S(1)}, f32[144,512]{1,0:T(8,128)S(1)}, u32[]{:S(2)}, u32[]{:S(2)}) %collective-permute-start.4) | collective-permute-done | bytes 294944 | tf_op jit(solution)/shard_map/ppermute | solution.py:237
  30.9 3.5 %collective-permute-start.5 = (f32[144,512]{1,0:T(8,128)S(1)}, f32[144,512]{1,0:T(8,128)S(1)}, u32[]{:S(2)}, u32[]{:S(2)}) collective-permute-start(f32[144,512]{1,0:T(8,128)S(1)} %collective-permute-done.4.refs_6_), channel_id=1, source_target_pairs={{0,7},{1,0},{2,1},{3,2},{4,3},{5,4},{6,5},{7,6},{8,15},{9,8},{10,9... | collective-permute-start | bytes 884744 | tf_op jit(solution)/shard_map/ppermute | solution.py:237
  34.4 3.7 %collective-permute-done.5.refs_7_ = f32[144,512]{1,0:T(8,128)S(1)} collective-permute-done((f32[144,512]{1,0:T(8,128)S(1)}, f32[144,512]{1,0:T(8,128)S(1)}, u32[]{:S(2)}, u32[]{:S(2)}) %collective-permute-start.5) | collective-permute-done | bytes 294944 | tf_op jit(solution)/shard_map/ppermute | solution.py:237
  38.8 2.5 %collective-permute-done.2.refs_3_ = f32[144,512]{1,0:T(8,128)} collective-permute-done((f32[144,512]{1,0:T(8,128)S(1)}, f32[144,512]{1,0:T(8,128)}, u32[]{:S(2)}, u32[]{:S(2)}) %collective-permute-start.2) | collective-permute-done | bytes 294944 | tf_op jit(solution)/shard_map/ppermute | solution.py:237
  41.3 1.0 all-to-all-done.refs_8_
  42.3 3.0 %collective-permute-start.7 = (f32[16,2,128,128]{3,2,1,0:T(8,128)}, f32[16,2,128,128]{3,2,1,0:T(8,128)}, u32[]{:S(2)}, u32[]{:S(2)}) collective-permute-start(f32[16,2,128,128]{3,2,1,0:T(8,128)} %all-to-all-done.refs_8_), channel_id=1, source_target_pairs={{0,8},{8,0},{16,24},{24,16},{32,40},{40,32},{48,56},{56,48},{64,72... | collective-permute-start | bytes 6291464 | tf_op jit(solution)/shard_map/ppermute | solution.py:269
  46.7 5.4 %all-to-all-start.1 = ((f32[16,4,64,128]{3,2,1,0:T(8,128)}), f32[16,4,64,128]{3,2,1,0:T(8,128)S(1)}, u32[]{:S(2)}, u32[]{:S(2)}) async-start(f32[16,4,64,128]{3,2,1,0:T(8,128)} %get-tuple-element.23), calls=%async_computation.1 | async-start | bytes 4194304 | tf_op jit(solution)/shard_map/all_to_all | solution.py:270
  52.2 5.6 %collective-permute-done.6.refs_4_ = f32[144,512]{1,0:T(8,128)} collective-permute-done((f32[144,512]{1,0:T(8,128)}, f32[144,512]{1,0:T(8,128)}, u32[]{:S(2)}, u32[]{:S(2)}) %collective-permute-start.6) | collective-permute-done | bytes 294944 | tf_op jit(solution)/shard_map/ppermute | solution.py:237
  57.7 5.2 %shard_map.104 = (f32[128,256]{1,0:T(8,128)}, f32[8,1,512]{2,1,0:T(1,128)}) custom-call(s32[3]{0:T(128)} %pad_add_fusion.ids, f32[144,512]{1,0:T(8,128)} %get-tuple-element.16.refs_0_, f32[144,512]{1,0:T(8,128)} %copy-done.4, f32[144,512]{1,0:T(8,128)} %copy-done.6, f32[144,512]{1,0:T(8,128)} %collective-permute-done.2.refs_3_, ...), custom_call_target="tpu_custom_call" | custom-call | flops 40000000000 | bytes 6000000 | tf_op jit(solution)/shard_map/pallas_call | solution.py:274
  62.9 1.8 %collective-permute-start.11 = (f32[128,256]{1,0:T(8,128)}, f32[128,256]{1,0:T(8,128)S(1)}, u32[]{:S(2)}, u32[]{:S(2)}) collective-permute-start(f32[128,256]{1,0:T(8,128)} %get-tuple-element.24.refs_10_), channel_id=1, source_target_pairs={{0,6},{1,7},{2,0},{3,1},{4,2},{5,3},{6,4},{7,5},{8,14},{9,15},{10,... | collective-permute-start | bytes 393224 | tf_op jit(solution)/shard_map/ppermute | solution.py:237
  65.3 3.8 %collective-permute-start.12 = (f32[128,256]{1,0:T(8,128)}, f32[128,256]{1,0:T(8,128)S(1)}, u32[]{:S(2)}, u32[]{:S(2)}) collective-permute-start(f32[128,256]{1,0:T(8,128)} %get-tuple-element.24.refs_10_), channel_id=1, source_target_pairs={{0,4},{1,5},{2,6},{3,7},{4,0},{5,1},{6,2},{7,3},{8,12},{9,13},{10,... | collective-permute-start | bytes 393224 | tf_op jit(solution)/shard_map/ppermute | solution.py:237
  69.6 1.0 collective-permute-start.8
  70.7 3.0 %collective-permute-start.14 = (f32[128,256]{1,0:T(8,128)S(1)}, f32[128,256]{1,0:T(8,128)S(1)}, u32[]{:S(2)}, u32[]{:S(2)}) collective-permute-start(f32[128,256]{1,0:T(8,128)S(1)} %collective-permute-done.11.refs_14_), channel_id=1, source_target_pairs={{0,7},{1,0},{2,1},{3,2},{4,3},{5,4},{6,5},{7,6},{8,15},{9,8},{10,9... | collective-permute-start | bytes 393224 | tf_op jit(solution)/shard_map/ppermute | solution.py:237
  74.1 11.4 %all-to-all-done.1.refs_8_ = f32[16,4,64,128]{3,2,1,0:T(8,128)S(1)} async-done(((f32[16,4,64,128]{3,2,1,0:T(8,128)}), f32[16,4,64,128]{3,2,1,0:T(8,128)S(1)}, u32[]{:S(2)}, u32[]{:S(2)}) %all-to-all-start.1) | async-done | bytes 2097184 | tf_op jit(solution)/shard_map/all_to_all | solution.py:270
  86.8 3.8 %collective-permute-done.15.refs_9_ = f32[16,4,64,128]{3,2,1,0:T(8,128)S(1)} collective-permute-done((f32[16,4,64,128]{3,2,1,0:T(8,128)S(1)}, f32[16,4,64,128]{3,2,1,0:T(8,128)S(1)}, u32[]{:S(2)}, u32[]{:S(2)}) %collective-permute-start.15) | collective-permute-done | bytes 2097184 | tf_op jit(solution)/shard_map/ppermute | solution.py:291
  90.6 1.3 %copy-done.1 = f32[16,4,64,128]{3,2,1,0:T(8,128)} copy-done((f32[16,4,64,128]{3,2,1,0:T(8,128)}, f32[16,4,64,128]{3,2,1,0:T(8,128)S(1)}, u32[]{:S(2)}) %copy-start.1) | copy-done | bytes 2097176
  92.0 8.6 %shard_map.105 = f32[32,8,128]{2,1,0:T(8,128)} custom-call(s32[3]{0:T(128)} %pad_add_fusion.ids, s32[4]{0:T(128)} %parents.1, s32[4]{0:T(128)} %widths.1, s32[4,64]{1,0:T(4,128)} %blocks.1, f32[4,32,128]{2,1,0:T(8,128)} %child_inv.1, f32[8,1,512]{2,1,0:T(1,128)} %get-tuple-element.22.root, f32[144,512]{1,0:T(8,128)} %get-tuple-element.16.refs_0_, ...), custom_call_target="tpu_custom_call" | custom-call | flops 2000000000 | bytes 10000000 | tf_op jit(solution)/shard_map/pallas_call | solution.py:293
  100.6 12.3 %all_to_all.15.parts = f32[32,8,128]{2,1,0:T(8,128)} all-to-all(f32[32,8,128]{2,1,0:T(8,128)} %shard_map.105), channel_id=1, replica_groups=mesh['row'=32,'col'=8] {'row'}, dimensions={0} | all-to-all | bytes 262144 | tf_op jit(solution)/shard_map/all_to_all | solution.py:317
  112.9 1.8 %shard_map.106 = (f32[1,128]{1,0:T(1,128)}, f32[2,32]{1,0:T(2,128)}, f32[4,128]{1,0:T(4,128)}) custom-call(s32[3]{0:T(128)} %pad_add_fusion.ids, f32[32,8,128]{2,1,0:T(8,128)} %all_to_all.15.parts), custom_call_target="tpu_custom_call" | custom-call | bytes 130000 | tf_op jit(solution)/shard_map/pallas_call | solution.py:314
  (48 shorter events, 5.1 us)
Async XLA Ops:
  4.0 38.3 %all-to-all-start = ((f32[16,2,128,128]{3,2,1,0:T(8,128)}), f32[16,2,128,128]{3,2,1,0:T(8,128)}, u32[]{:S(2)}, u32[]{:S(2)}) async-start(f32[16,2,128,128]{3,2,1,0:T(8,128)} %get-tuple-element.17), calls=%async_computation | async-start | bytes 4194304 | tf_op jit(solution)/shard_map/all_to_all | solution.py:264
  11.8 11.0 %collective-permute-start.3 = (f32[144,512]{1,0:T(8,128)S(1)}, f32[144,512]{1,0:T(8,128)S(1)}, u32[]{:S(2)}, u32[]{:S(2)}) collective-permute-start(f32[144,512]{1,0:T(8,128)S(1)} %copy-done.2), channel_id=1, source_target_pairs={{0,7},{1,0},{2,1},{3,2},{4,3},{5,4},{6,5},{7,6},{8,15},{9,8},{10,9... | collective-permute-start | bytes 884744 | tf_op jit(solution)/shard_map/ppermute | solution.py:237
  17.4 8.9 %collective-permute-start = (f32[144,512]{1,0:T(8,128)S(1)}, f32[144,512]{1,0:T(8,128)S(1)}, u32[]{:S(2)}, u32[]{:S(2)}) collective-permute-start(f32[144,512]{1,0:T(8,128)S(1)} %copy-done.2), channel_id=1, source_target_pairs={{0,1},{1,2},{2,3},{3,4},{4,5},{5,6},{6,7},{7,0},{8,9},{9,10},{10,1... | collective-permute-start | bytes 884744 | tf_op jit(solution)/shard_map/ppermute | solution.py:237
  22.8 23.9 %copy-start.3 = (f32[144,512]{1,0:T(8,128)}, f32[144,512]{1,0:T(8,128)S(1)}, u32[]{:S(2)}) copy-start(f32[144,512]{1,0:T(8,128)S(1)} %collective-permute-done.3.refs_5_) | copy-start | bytes 884740
  22.8 8.1 %collective-permute-start.4 = (f32[144,512]{1,0:T(8,128)S(1)}, f32[144,512]{1,0:T(8,128)S(1)}, u32[]{:S(2)}, u32[]{:S(2)}) collective-permute-start(f32[144,512]{1,0:T(8,128)S(1)} %collective-permute-done.3.refs_5_), channel_id=1, source_target_pairs={{0,7},{1,0},{2,1},{3,2},{4,3},{5,4},{6,5},{7,6},{8,15},{9,8},{10,9... | collective-permute-start | bytes 884744 | tf_op jit(solution)/shard_map/ppermute | solution.py:237
  26.3 20.4 %copy-start.4 = (f32[144,512]{1,0:T(8,128)}, f32[144,512]{1,0:T(8,128)S(1)}, u32[]{:S(2)}) copy-start(f32[144,512]{1,0:T(8,128)S(1)} %collective-permute-done.refs_1_) | copy-start | bytes 884740
  26.3 8.1 %collective-permute-start.1 = (f32[144,512]{1,0:T(8,128)S(1)}, f32[144,512]{1,0:T(8,128)S(1)}, u32[]{:S(2)}, u32[]{:S(2)}) collective-permute-start(f32[144,512]{1,0:T(8,128)S(1)} %collective-permute-done.refs_1_), channel_id=1, source_target_pairs={{0,1},{1,2},{2,3},{3,4},{4,5},{5,6},{6,7},{7,0},{8,9},{9,10},{10,1... | collective-permute-start | bytes 884744 | tf_op jit(solution)/shard_map/ppermute | solution.py:237
  30.9 15.9 %copy-start.5 = (f32[144,512]{1,0:T(8,128)}, f32[144,512]{1,0:T(8,128)S(1)}, u32[]{:S(2)}) copy-start(f32[144,512]{1,0:T(8,128)S(1)} %collective-permute-done.4.refs_6_) | copy-start | bytes 884740
  30.9 7.2 %collective-permute-start.5 = (f32[144,512]{1,0:T(8,128)S(1)}, f32[144,512]{1,0:T(8,128)S(1)}, u32[]{:S(2)}, u32[]{:S(2)}) collective-permute-start(f32[144,512]{1,0:T(8,128)S(1)} %collective-permute-done.4.refs_6_), channel_id=1, source_target_pairs={{0,7},{1,0},{2,1},{3,2},{4,3},{5,4},{6,5},{7,6},{8,15},{9,8},{10,9... | collective-permute-start | bytes 884744 | tf_op jit(solution)/shard_map/ppermute | solution.py:237
  34.4 12.3 %copy-start.6 = (f32[144,512]{1,0:T(8,128)}, f32[144,512]{1,0:T(8,128)S(1)}, u32[]{:S(2)}) copy-start(f32[144,512]{1,0:T(8,128)S(1)} %collective-permute-done.1.refs_2_) | copy-start | bytes 884740
  34.4 6.9 %collective-permute-start.2 = (f32[144,512]{1,0:T(8,128)S(1)}, f32[144,512]{1,0:T(8,128)}, u32[]{:S(2)}, u32[]{:S(2)}) collective-permute-start(f32[144,512]{1,0:T(8,128)S(1)} %collective-permute-done.1.refs_2_), channel_id=1, source_target_pairs={{0,1},{1,2},{2,3},{3,4},{4,5},{5,6},{6,7},{7,0},{8,9},{9,10},{10,1... | collective-permute-start | bytes 884744 | tf_op jit(solution)/shard_map/ppermute | solution.py:237
  42.3 15.4 %collective-permute-start.7 = (f32[16,2,128,128]{3,2,1,0:T(8,128)}, f32[16,2,128,128]{3,2,1,0:T(8,128)}, u32[]{:S(2)}, u32[]{:S(2)}) collective-permute-start(f32[16,2,128,128]{3,2,1,0:T(8,128)} %all-to-all-done.refs_8_), channel_id=1, source_target_pairs={{0,8},{8,0},{16,24},{24,16},{32,40},{40,32},{48,56},{56,48},{64,72... | collective-permute-start | bytes 6291464 | tf_op jit(solution)/shard_map/ppermute | solution.py:269
  45.3 12.4 %collective-permute-start.6 = (f32[144,512]{1,0:T(8,128)}, f32[144,512]{1,0:T(8,128)}, u32[]{:S(2)}, u32[]{:S(2)}) collective-permute-start(f32[144,512]{1,0:T(8,128)} %collective-permute-done.2.refs_3_), channel_id=1, source_target_pairs={{0,1},{1,2},{2,3},{3,4},{4,5},{5,6},{6,7},{7,0},{8,9},{9,10},{10,1... | collective-permute-start | bytes 884744 | tf_op jit(solution)/shard_map/ppermute | solution.py:237
  46.7 38.8 %all-to-all-start.1 = ((f32[16,4,64,128]{3,2,1,0:T(8,128)}), f32[16,4,64,128]{3,2,1,0:T(8,128)S(1)}, u32[]{:S(2)}, u32[]{:S(2)}) async-start(f32[16,4,64,128]{3,2,1,0:T(8,128)} %get-tuple-element.23), calls=%async_computation.1 | async-start | bytes 4194304 | tf_op jit(solution)/shard_map/all_to_all | solution.py:270
  62.9 7.8 %collective-permute-start.11 = (f32[128,256]{1,0:T(8,128)}, f32[128,256]{1,0:T(8,128)S(1)}, u32[]{:S(2)}, u32[]{:S(2)}) collective-permute-start(f32[128,256]{1,0:T(8,128)} %get-tuple-element.24.refs_10_), channel_id=1, source_target_pairs={{0,6},{1,7},{2,0},{3,1},{4,2},{5,3},{6,4},{7,5},{8,14},{9,15},{10,... | collective-permute-start | bytes 393224 | tf_op jit(solution)/shard_map/ppermute | solution.py:237
  64.7 9.4 %collective-permute-start.10 = (f32[128,256]{1,0:T(8,128)}, f32[128,256]{1,0:T(8,128)S(1)}, u32[]{:S(2)}, u32[]{:S(2)}) collective-permute-start(f32[128,256]{1,0:T(8,128)} %get-tuple-element.24.refs_10_), channel_id=1, source_target_pairs={{0,2},{1,3},{2,4},{3,5},{4,6},{5,7},{6,0},{7,1},{8,10},{9,11},{10,... | collective-permute-start | bytes 393224 | tf_op jit(solution)/shard_map/ppermute | solution.py:237
  65.3 20.2 %collective-permute-start.12 = (f32[128,256]{1,0:T(8,128)}, f32[128,256]{1,0:T(8,128)S(1)}, u32[]{:S(2)}, u32[]{:S(2)}) collective-permute-start(f32[128,256]{1,0:T(8,128)} %get-tuple-element.24.refs_10_), channel_id=1, source_target_pairs={{0,4},{1,5},{2,6},{3,7},{4,0},{5,1},{6,2},{7,3},{8,12},{9,13},{10,... | collective-permute-start | bytes 393224 | tf_op jit(solution)/shard_map/ppermute | solution.py:237
  69.1 16.4 %collective-permute-start.9 = (f32[128,256]{1,0:T(8,128)}, f32[128,256]{1,0:T(8,128)S(1)}, u32[]{:S(2)}, u32[]{:S(2)}) collective-permute-start(f32[128,256]{1,0:T(8,128)} %get-tuple-element.24.refs_10_), channel_id=1, source_target_pairs={{0,7},{1,0},{2,1},{3,2},{4,3},{5,4},{6,5},{7,6},{8,15},{9,8},{10,9... | collective-permute-start | bytes 393224 | tf_op jit(solution)/shard_map/ppermute | solution.py:237
  69.6 16.0 %collective-permute-start.8 = (f32[128,256]{1,0:T(8,128)}, f32[128,256]{1,0:T(8,128)S(1)}, u32[]{:S(2)}, u32[]{:S(2)}) collective-permute-start(f32[128,256]{1,0:T(8,128)} %get-tuple-element.24.refs_10_), channel_id=1, source_target_pairs={{0,1},{1,2},{2,3},{3,4},{4,5},{5,6},{6,7},{7,0},{8,9},{9,10},{10,1... | collective-permute-start | bytes 393224 | tf_op jit(solution)/shard_map/ppermute | solution.py:237
  70.7 21.3 %copy-start.8 = (f32[128,256]{1,0:T(8,128)}, f32[128,256]{1,0:T(8,128)S(1)}, u32[]{:S(2)}) copy-start(f32[128,256]{1,0:T(8,128)S(1)} %collective-permute-done.11.refs_14_) | copy-start | bytes 393220
  70.7 14.9 %collective-permute-start.14 = (f32[128,256]{1,0:T(8,128)S(1)}, f32[128,256]{1,0:T(8,128)S(1)}, u32[]{:S(2)}, u32[]{:S(2)}) collective-permute-start(f32[128,256]{1,0:T(8,128)S(1)} %collective-permute-done.11.refs_14_), channel_id=1, source_target_pairs={{0,7},{1,0},{2,1},{3,2},{4,3},{5,4},{6,5},{7,6},{8,15},{9,8},{10,9... | collective-permute-start | bytes 393224 | tf_op jit(solution)/shard_map/ppermute | solution.py:237
  74.1 17.8 %copy-start.9 = (f32[128,256]{1,0:T(8,128)}, f32[128,256]{1,0:T(8,128)S(1)}, u32[]{:S(2)}) copy-start(f32[128,256]{1,0:T(8,128)S(1)} %collective-permute-done.10.refs_13_) | copy-start | bytes 393220
  74.1 11.8 %collective-permute-start.13 = (f32[128,256]{1,0:T(8,128)S(1)}, f32[128,256]{1,0:T(8,128)S(1)}, u32[]{:S(2)}, u32[]{:S(2)}) collective-permute-start(f32[128,256]{1,0:T(8,128)S(1)} %collective-permute-done.10.refs_13_), channel_id=1, source_target_pairs={{0,1},{1,2},{2,3},{3,4},{4,5},{5,6},{6,7},{7,0},{8,9},{9,10},{10,1... | collective-permute-start | bytes 393224 | tf_op jit(solution)/shard_map/ppermute | solution.py:237
  86.0 4.7 %collective-permute-start.15 = (f32[16,4,64,128]{3,2,1,0:T(8,128)S(1)}, f32[16,4,64,128]{3,2,1,0:T(8,128)S(1)}, u32[]{:S(2)}, u32[]{:S(2)}) collective-permute-start(f32[16,4,64,128]{3,2,1,0:T(8,128)S(1)} %all-to-all-done.1.refs_8_), channel_id=1, source_target_pairs={{0,8},{8,0},{16,24},{24,16},{32,40},{40,32},{48,56},{56,48},{64,72... | collective-permute-start | bytes 6291464 | tf_op jit(solution)/shard_map/ppermute | solution.py:291
  (9 other events, 47.9 us)
